TPU v7x, 256 devices: a whole 4x4x8 slice. The times are simulated.
256 devices in a mesh: sec: 4 (over y), ctx: 16 (over z, x_hi), tp: 4 (over x_lo, core).
Axes of the slice: x: 4 (x_hi: 2, x_lo: 2; x = x_hi * 2 + x_lo), y: 4, z: 8, core: 2. Of those that a mesh axis runs over, the one named last changes fastest.
Arguments:
- self_query: bfloat16 [8192, 2048], P('ctx', ('sec', 'tp')), may hold values from -6 to 6
- self_key: bfloat16 [8192, 2048], P('ctx', ('sec', 'tp')), may hold values from -6 to 6
- self_value: bfloat16 [8192, 2048], P('ctx', ('sec', 'tp')), may hold values from -6 to 6
- self_gain: float32 [2048], P(('sec', 'tp')), may hold values from 0.5 to 1.5
- self_grad: bfloat16 [8192, 2048], P('ctx', ('sec', 'tp')), may hold values from -6 to 6
- cross_query: bfloat16 [8192, 2048], P('ctx', ('sec', 'tp')), may hold values from -6 to 6
- memory_key: bfloat16 [2048, 2048], P(('sec', 'ctx')), may hold values from -6 to 6
- memory_value: bfloat16 [2048, 2048], P(('sec', 'ctx')), may hold values from -6 to 6
- cross_gain: float32 [2048], P(('sec', 'tp')), may hold values from 0.5 to 1.5
- cross_grad: bfloat16 [8192, 2048], P('ctx', ('sec', 'tp')), may hold values from -6 to 6
- block_start: int32 [64], replicated, may hold values from 0 to 63, each once
Outputs:
- self_out: bfloat16 [8192, 2048], P('ctx', ('sec', 'tp'))
- cross_out: bfloat16 [8192, 2048], P('ctx', ('sec', 'tp'))
- query_grad: bfloat16 [8192, 2048], P('ctx', ('sec', 'tp'))
- key_grad: bfloat16 [8192, 2048], P('ctx', ('sec', 'tp'))
- value_grad: bfloat16 [8192, 2048], P('ctx', ('sec', 'tp'))
- cross_query_grad: bfloat16 [8192, 2048], P('ctx', ('sec', 'tp'))
- memory_key_grad: bfloat16 [2048, 2048], P(('sec', 'ctx'))
- memory_value_grad: bfloat16 [2048, 2048], P(('sec', 'ctx'))
Inputs may be any that keep to these rules, and one draw needn't show every extreme that they name: `block_start`: every number appears once.
All inputs are finite; a program needn't handle non-finite values.
Results may differ from a plain program's by a relative error of at most 0.015.
Values may be sent and summed in bfloat16 or wider, within the bound.
A program may use at most 64 MiB of HBM per device.

v0:
```python
import math

import jax
import jax.numpy as jnp
from jax import lax
from jax.sharding import PartitionSpec as P

HEADS = 16
HEAD_DIM = 128


EPS = 1e-06
NEG_FILL = -1e30


def in_one_piece(arrays, axis, dim, along):
    ends, at = ([], 0)
    for a in arrays[:-1]:
        at += a.shape[along]
        ends.append(at)
    both = jnp.concatenate(arrays, axis=along)
    return tuple(jnp.split(lax.all_gather(both, axis, axis=dim, tiled=True), ends, axis=along))


def sent_to_all(array, axis):
    copies = jnp.broadcast_to(array, (lax.axis_size(axis), *array.shape))
    return lax.all_to_all(copies, axis, split_axis=0, concat_axis=0, tiled=True)


def of_everyone(array, axis):
    return sent_to_all(array, axis).sum(axis=0)


def in_one(arrays, axis):
    ends = [0]
    for a in arrays:
        ends.append(ends[-1] + a.size)
    running = of_everyone(jnp.concatenate([a.ravel() for a in arrays]), axis)
    return tuple((running[b:e].reshape(a.shape) for a, b, e in zip(arrays, ends, ends[1:])))


def in_blocks(array, dim, count):
    dims = array.shape
    parts = array.reshape(*dims[:dim], count, dims[dim] // count, *dims[dim + 1 :])
    return jnp.moveaxis(parts, dim, 0)


def sent_and_summed(array, axis, dim):
    parts = in_blocks(array, dim, lax.axis_size(axis))
    arrived = lax.all_to_all(parts, axis, split_axis=0, concat_axis=0, tiled=True)
    return arrived.astype(jnp.float32).sum(axis=0)


def split_heads(matrix):
    return matrix.reshape(matrix.shape[0], matrix.shape[1] // HEAD_DIM, HEAD_DIM)


def frame_positions(block_start, first_row, row_count, block_rows):
    row_ids = first_row + jnp.arange(row_count, dtype=jnp.int32)
    owners = row_ids // block_rows
    lookup = owners[:, None] == jnp.arange(block_start.shape[0], dtype=jnp.int32)[None, :]
    starts = jnp.sum(jnp.where(lookup, block_start[None, :], 0), axis=1)
    return starts * block_rows + row_ids % block_rows


def skipped(key_positions, query_positions):
    return jnp.min(key_positions) > jnp.max(query_positions)


def masked_scores(queries, key_block, key_positions, query_positions, filler):
    scores = jnp.einsum("qhd,khd->hqk", queries, key_block, preferred_element_type=jnp.float32) * (
        1.0 / math.sqrt(HEAD_DIM)
    )
    if key_positions is None:
        return scores
    return jnp.where(key_positions[None, None, :] > query_positions[None, :, None], filler, scores)


def fold_softmax(carried, pieces, queries, query_positions, position_of):
    row_top, row_total, key_store, value_store = carried
    key_piece, value_piece = pieces
    row_count = key_piece.shape[0]
    key_store = key_piece
    value_store = value_piece
    block_length = math.gcd(row_count, 1024)

    def fold_visit(turn_index, running):
        offset = turn_index * block_length
        key_block = split_heads(lax.dynamic_slice_in_dim(key_piece, offset, block_length, 0))
        key_positions = None if position_of is None else position_of(offset, block_length)

        def fold_update(current):
            old_top, old_total = current
            scores = masked_scores(queries, key_block, key_positions, query_positions, NEG_FILL)
            new_top = jnp.maximum(old_top, jnp.max(scores, axis=2))
            new_total = old_total * jnp.exp(old_top - new_top) + jnp.sum(
                jnp.exp(scores - new_top[:, :, None]), axis=2
            )
            return (new_top, new_total)

        if key_positions is None:
            return fold_update(running)
        return lax.cond(
            skipped(key_positions, query_positions), lambda unused: unused, fold_update, running
        )

    row_top, row_total = lax.fori_loop(
        0, row_count // block_length, fold_visit, (row_top, row_total)
    )
    return (row_top, row_total, key_store, value_store)


def attend(queries, log_total, key_store, value_store, query_positions, position_of):
    key_count = key_store.shape[0]
    block_length = math.gcd(key_count, 512)

    def attend_visit(turn_index, running):
        offset = turn_index * block_length
        key_block = split_heads(lax.dynamic_slice_in_dim(key_store, offset, block_length, 0))
        value_block = split_heads(lax.dynamic_slice_in_dim(value_store, offset, block_length, 0))
        key_positions = None if position_of is None else position_of(offset, block_length)

        def attend_update(current):
            scores = masked_scores(queries, key_block, key_positions, query_positions, -jnp.inf)
            weights = jnp.exp(scores - log_total[:, :, None]).astype(jnp.bfloat16)
            return current + jnp.einsum(
                "hqk,khd->qhd", weights, value_block, preferred_element_type=jnp.float32
            )

        if key_positions is None:
            return attend_update(running)
        return lax.cond(
            skipped(key_positions, query_positions), lambda unused: unused, attend_update, running
        )

    result = lax.fori_loop(
        0, key_count // block_length, attend_visit, jnp.zeros(queries.shape, jnp.float32)
    )
    return result.reshape(queries.shape[0], queries.shape[1] * HEAD_DIM)


def score_parts(
    queries, cotangent, log_total, row_delta, key_block, value_block, key_positions, query_positions
):
    scores = masked_scores(queries, key_block, key_positions, query_positions, -jnp.inf)
    weights = jnp.exp(scores - log_total[:, :, None])
    products = jnp.einsum(
        "qhd,khd->hqk", cotangent, value_block, preferred_element_type=jnp.float32
    )
    score_grad = (weights * (products - row_delta[:, :, None])).astype(jnp.bfloat16)
    return (weights, score_grad)


def key_side_terms(queries, cotangent, weights, score_grad):
    key_part = jnp.einsum(
        "hqk,qhd->khd", score_grad, queries, preferred_element_type=jnp.float32
    ) * (1.0 / math.sqrt(HEAD_DIM))
    value_part = jnp.einsum(
        "hqk,qhd->khd", weights.astype(jnp.bfloat16), cotangent, preferred_element_type=jnp.float32
    )
    rows_here = key_part.shape[0]
    return jnp.concatenate(
        [key_part.reshape(rows_here, -1), value_part.reshape(rows_here, -1)], axis=1
    )


def query_grads(
    queries, cotangent, log_total, row_delta, key_store, value_store, query_positions, position_of
):
    key_count = key_store.shape[0]
    block_length = math.gcd(key_count, 512)

    def query_visit(turn_index, running):
        offset = turn_index * block_length
        key_block = split_heads(lax.dynamic_slice_in_dim(key_store, offset, block_length, 0))
        value_block = split_heads(lax.dynamic_slice_in_dim(value_store, offset, block_length, 0))
        key_positions = position_of(offset, block_length)

        def query_update(current):
            weights, score_grad = score_parts(
                queries,
                cotangent,
                log_total,
                row_delta,
                key_block,
                value_block,
                key_positions,
                query_positions,
            )
            return current + jnp.einsum(
                "hqk,khd->qhd", score_grad, key_block, preferred_element_type=jnp.float32
            ) * (1.0 / math.sqrt(HEAD_DIM))

        return lax.cond(
            skipped(key_positions, query_positions), lambda unused: unused, query_update, running
        )

    result = lax.fori_loop(
        0, key_count // block_length, query_visit, jnp.zeros(queries.shape, jnp.float32)
    )
    return result.reshape(queries.shape[0], queries.shape[1] * HEAD_DIM)


def joint_backward(queries, cotangent, log_total, row_delta, key_store, value_store):
    key_count = key_store.shape[0]
    block_length = math.gcd(key_count, 512)
    columns = queries.shape[1] * HEAD_DIM

    def joint_visit(turn_index, running):
        offset = turn_index * block_length
        key_block = split_heads(lax.dynamic_slice_in_dim(key_store, offset, block_length, 0))
        value_block = split_heads(lax.dynamic_slice_in_dim(value_store, offset, block_length, 0))
        key_positions = None
        query_sum, key_terms = running
        weights, score_grad = score_parts(
            queries, cotangent, log_total, row_delta, key_block, value_block, key_positions, None
        )
        query_sum = query_sum + jnp.einsum(
            "hqk,khd->qhd", score_grad, key_block, preferred_element_type=jnp.float32
        ) * (1.0 / math.sqrt(HEAD_DIM))
        key_terms = lax.dynamic_update_slice_in_dim(
            key_terms, key_side_terms(queries, cotangent, weights, score_grad), offset, 0
        )
        return (query_sum, key_terms)

    start_value = (
        jnp.zeros(queries.shape, jnp.float32),
        jnp.zeros((key_count, 2 * columns), jnp.float32),
    )
    query_sum, key_terms = lax.fori_loop(0, key_count // block_length, joint_visit, start_value)
    return (query_sum.reshape(queries.shape[0], columns), key_terms)


def backprop_norm(attended, lifted, row_scale, row_slope):
    return (
        row_scale[:, None] * (lifted - attended * (row_scale * row_scale * row_slope)[:, None])
    ).astype(jnp.bfloat16)


def head_delta(attended_grad, attended):
    return jnp.sum(
        (attended_grad.astype(jnp.float32) * attended).reshape(attended.shape[0], -1, HEAD_DIM),
        axis=2,
    ).T


def per_device(
    self_query,
    self_key,
    self_value,
    self_gain,
    self_grad,
    cross_query,
    memory_key,
    memory_value,
    cross_gain,
    cross_grad,
    block_start,
):
    frames_dev, columns = self_query.shape
    quarter_rows = frames_dev // 4
    full_width = HEADS * HEAD_DIM
    context_count = lax.axis_size("ctx")
    section_count = lax.axis_size("sec")
    tensor_count = lax.axis_size("tp")
    memory_rows = memory_key.shape[0]
    head_count = columns // HEAD_DIM
    own_positions = frame_positions(
        block_start, lax.axis_index("ctx") * frames_dev, frames_dev, quarter_rows
    )

    def position_of(first_row, row_count):
        return frame_positions(block_start, first_row, row_count, quarter_rows)

    own_queries = split_heads(self_query)
    empty_top = jnp.full((head_count, frames_dev), NEG_FILL, jnp.float32)
    empty_total = jnp.zeros((head_count, frames_dev), jnp.float32)
    frame_store = jnp.zeros((frames_dev * context_count, columns), jnp.bfloat16)
    self_top, self_sum, key_store, value_store = fold_softmax(
        (empty_top, empty_total, frame_store, frame_store),
        in_one_piece((self_key, self_value), "ctx", 0, 1),
        own_queries,
        own_positions,
        position_of,
    )
    self_log_total = self_top + jnp.log(self_sum)
    self_attended = attend(
        own_queries, self_log_total, key_store, value_store, own_positions, position_of
    )

    def own_heads(memory):
        grouped = memory.reshape(memory_rows, section_count, tensor_count, columns)
        picked = lax.dynamic_slice_in_dim(grouped, lax.axis_index("tp"), 1, 2)
        return picked.reshape(memory_rows, section_count, columns)

    memory_keys, memory_values = (
        lax.all_to_all(own_heads(memory_key), "sec", split_axis=1, concat_axis=0, tiled=True),
        lax.all_to_all(own_heads(memory_value), "sec", split_axis=1, concat_axis=0, tiled=True),
    )
    section_rows = section_count * memory_rows
    memory_keys = memory_keys.reshape(section_rows, columns)
    memory_values = memory_values.reshape(section_rows, columns)
    cross_queries = split_heads(cross_query)
    memory_store = jnp.zeros((section_rows * context_count, columns), jnp.bfloat16)
    cross_top, cross_sum, memory_key_store, memory_value_store = fold_softmax(
        (empty_top, empty_total, memory_store, memory_store),
        (
            lax.all_gather(memory_keys, "ctx", axis=0, tiled=True),
            lax.all_gather(memory_values, "ctx", axis=0, tiled=True),
        ),
        cross_queries,
        own_positions,
        None,
    )
    cross_log_total = cross_top + jnp.log(cross_sum)
    cross_attended = attend(
        cross_queries, cross_log_total, memory_key_store, memory_value_store, own_positions, None
    )
    self_lifted = self_gain[None, :] * self_grad.astype(jnp.float32)
    cross_lifted = cross_gain[None, :] * cross_grad.astype(jnp.float32)
    self_squares = jnp.sum(self_attended * self_attended, axis=1)
    cross_squares = jnp.sum(cross_attended * cross_attended, axis=1)
    self_square_sum, cross_square_sum, self_slope_sum, cross_slope_sum = in_one(
        (
            self_squares,
            cross_squares,
            jnp.sum(self_lifted * self_attended, axis=1),
            jnp.sum(cross_lifted * cross_attended, axis=1),
        ),
        ("sec", "tp"),
    )
    self_scale = lax.rsqrt(self_square_sum / full_width + EPS)
    cross_scale = lax.rsqrt(cross_square_sum / full_width + EPS)
    self_out = (self_gain[None, :] * self_attended * self_scale[:, None]).astype(jnp.bfloat16)
    cross_out = (cross_gain[None, :] * cross_attended * cross_scale[:, None]).astype(jnp.bfloat16)
    self_attended_grad = backprop_norm(
        self_attended, self_lifted, self_scale, self_slope_sum / full_width
    )
    cross_attended_grad = backprop_norm(
        cross_attended, cross_lifted, cross_scale, cross_slope_sum / full_width
    )
    self_delta = head_delta(self_attended_grad, self_attended)
    self_cotangent = split_heads(self_attended_grad)
    query_grad = query_grads(
        own_queries,
        self_cotangent,
        self_log_total,
        self_delta,
        key_store,
        value_store,
        own_positions,
        position_of,
    ).astype(jnp.bfloat16)
    all_log_total, all_delta = in_one_piece((self_log_total.T, self_delta.T), "ctx", 0, 1)
    own_keys = split_heads(self_key)
    own_values = split_heads(self_value)
    query_piece, grad_piece = in_one_piece((self_query, self_attended_grad), "ctx", 0, 1)
    row_count = query_piece.shape[0]
    block_length = math.gcd(row_count, 1024)

    def requery_visit(turn_index, running):
        offset = turn_index * block_length
        query_positions = position_of(offset, block_length)
        query_block = split_heads(lax.dynamic_slice_in_dim(query_piece, offset, block_length, 0))
        grad_block = split_heads(lax.dynamic_slice_in_dim(grad_piece, offset, block_length, 0))
        total_block = lax.dynamic_slice_in_dim(all_log_total, offset, block_length, 0).T
        delta_block = lax.dynamic_slice_in_dim(all_delta, offset, block_length, 0).T

        def requery_update(current):
            weights, score_grad = score_parts(
                query_block,
                grad_block,
                total_block,
                delta_block,
                own_keys,
                own_values,
                own_positions,
                query_positions,
            )
            return current + key_side_terms(query_block, grad_block, weights, score_grad)

        return lax.cond(
            skipped(own_positions, query_positions), lambda unused: unused, requery_update, running
        )

    key_terms = lax.fori_loop(
        0,
        row_count // block_length,
        requery_visit,
        jnp.zeros((frames_dev, 2 * columns), jnp.float32),
    )
    key_grad = key_terms[:, :columns].astype(jnp.bfloat16)
    value_grad = key_terms[:, columns:].astype(jnp.bfloat16)
    cross_delta = head_delta(cross_attended_grad, cross_attended)
    cross_query_sum, memory_terms = joint_backward(
        cross_queries,
        split_heads(cross_attended_grad),
        cross_log_total,
        cross_delta,
        memory_key_store,
        memory_value_store,
    )
    cross_query_grad = cross_query_sum.astype(jnp.bfloat16)
    memory_sums = sent_and_summed(memory_terms.astype(jnp.bfloat16), "ctx", 0)
    rounded = memory_sums.astype(jnp.bfloat16).reshape(section_rows, 2, 1, 1, columns)
    returned = lax.all_to_all(rounded, "sec", split_axis=0, concat_axis=2, tiled=True)
    complete = lax.all_gather(returned, "tp", axis=3, tiled=True).reshape(
        memory_rows, 2, section_count * tensor_count * columns
    )
    return (
        self_out,
        cross_out,
        query_grad,
        key_grad,
        value_grad,
        cross_query_grad,
        complete[:, 0],
        complete[:, 1],
    )


def solution(mesh):
    return jax.shard_map(
        per_device,
        mesh=mesh,
        in_specs=(
            P("ctx", ("sec", "tp")),
            P("ctx", ("sec", "tp")),
            P("ctx", ("sec", "tp")),
            P(("sec", "tp")),
            P("ctx", ("sec", "tp")),
            P("ctx", ("sec", "tp")),
            P(("sec", "ctx"), None),
            P(("sec", "ctx"), None),
            P(("sec", "tp")),
            P("ctx", ("sec", "tp")),
            P(),
        ),
        out_specs=(
            P("ctx", ("sec", "tp")),
            P("ctx", ("sec", "tp")),
            P("ctx", ("sec", "tp")),
            P("ctx", ("sec", "tp")),
            P("ctx", ("sec", "tp")),
            P("ctx", ("sec", "tp")),
            P(("sec", "ctx"), None),
            P(("sec", "ctx"), None),
        ),
        check_vma=False,
    )
```

profile of v0, /device:TPU:1, one launch (start us, length us, event | category | flops | bytes accessed | tf_op | source)
XLA Modules:
  0.0 478.1 jit_solution(1597466456560088338)
XLA Ops:
  10.7 5.0 %all-to-all-start.1 = ((bf16[32,4,128]{2,0,1:T(8,128)(2,1)}), bf16[32,4,128]{2,0,1:T(8,128)(2,1)S(1)}, u32[]{:S(2)}, u32[]{:S(2)}) async-start(bf16[32,4,128]{2,0,1:T(8,128)(2,1)} %bitcast.224), calls=%async_computation.1 | async-start | bytes 65536 | tf_op jit(solution)/shard_map/all_to_all | solution.py:297
  20.0 3.7 all-to-all-start
  23.7 41.2 %all_gather.20 = bf16[2048,128]{1,0:T(8,128)(2,1)S(1)} all-gather(bf16[128,128]{1,0:T(8,128)(2,1)S(1)} %bitcast.273), channel_id=1, replica_groups=mesh['sec'=4,'ctx'=16,'tp'=4] {'ctx'}, dimensions={0}, use_global_device_ids=true | all-gather | bytes 557056 | tf_op jit(solution)/shard_map/all_gather | solution.py:308
  66.7 36.3 %all_gather.19 = bf16[2048,128]{1,0:T(8,128)(2,1)S(1)} all-gather(bf16[128,128]{1,0:T(8,128)(2,1)S(1)} %bitcast.272), channel_id=1, replica_groups=mesh['sec'=4,'ctx'=16,'tp'=4] {'ctx'}, dimensions={0}, use_global_device_ids=true | all-gather | bytes 557056 | tf_op jit(solution)/shard_map/all_gather | solution.py:309
  105.8 14.9 %all-gather.4.cloned.1.call-done = bf16[8192,256]{1,0:T(8,128)(2,1)} async-done(((bf16[512,256]{1,0:T(8,128)(2,1)}), bf16[8192,256]{1,0:T(8,128)(2,1)}) %all-gather.4.cloned.1.call-update) | async-done | bytes 4194320 | tf_op jit(solution)/shard_map/all_gather | solution.py:22
  120.7 3.8 fusion.168
  125.1 37.2 %while.117 = (s32[]{:T(128)}, f32[1,512]{1,0:T(1,128)S(1)}, f32[1,512]{1,0:T(1,128)}, s32[64]{0:T(128)S(1)}, s32[]{:T(128)}, /*index=5*/s32[512]{0:T(512)}, bf16...) while((s32[]{:T(128)}, f32[1,512]{1,0:T(1,128)S(1)}, f32[1,512]{1,0:T(1,128)}, ...), condition=%wide.region_9.10_spmd, body=%wide.region_2.9_spmd.sunk | while | flops 139164672 | bytes 4672093 | solution.py:107
  163.7 70.9 %while.118 = (s32[]{:T(128)}, f32[512,1,128]{0,2,1:T(8,128)}, s32[64]{0:T(128)S(1)}, s32[]{:T(128)}, bf16[8192,128]{1,0:T(8,128)(2,1)}, /*index=5*/s32[512]{0:T(...) while((s32[]{:T(128)}, f32[512,1,128]{0,2,1:T(8,128)}, ...), condition=%wide.region_15.16_spmd, body=%wide.region_10.15_spmd.sunk | while | flops 135707648 | bytes 935421 | solution.py:136
  239.3 8.0 %all-to-all-start.2 = ((f32[16,1,2048]{2,1,0:T(1,128)}), f32[16,1,2048]{2,1,0:T(1,128)}, u32[]{:S(2)}, u32[]{:S(2)}) async-start(f32[16,1,2048]{2,1,0:T(1,128)} %broadcast_in_dim.223), calls=%async_computation.2 | async-start | bytes 262144 | tf_op jit(solution)/shard_map/all_to_all | solution.py:27
  247.4 6.2 %all-to-all-done.2 = f32[16,1,2048]{2,1,0:T(1,128)} async-done(((f32[16,1,2048]{2,1,0:T(1,128)}), f32[16,1,2048]{2,1,0:T(1,128)}, u32[]{:S(2)}, u32[]{:S(2)}) %all-to-all-start.2) | async-done | bytes 131104 | tf_op jit(solution)/shard_map/all_to_all | solution.py:27
  260.0 7.1 %while.123 = (s32[]{:T(128)}, f32[512,1,128]{0,2,1:T(8,128)S(1)}, bf16[2048,256]{1,0:T(8,128)(2,1)S(1)}, bf16[2048,128]{1,0:T(8,128)(2,1)S(1)}, bf16[512,1,128]{...) while((s32[]{:T(128)}, f32[512,1,128]{0,2,1:T(8,128)S(1)}, ...), condition=%wide.region_43.44_spmd.clone, body=%wide.region_42.43_spmd.clone.sunk | while | flops 337969152 | bytes 7999693 | solution.py:230
  268.5 6.0 %all-to-all-start.3 = ((bf16[16,128,256]{1,2,0:T(8,128)(2,1)}), bf16[16,128,256]{1,2,0:T(8,128)(2,1)S(1)}, u32[]{:S(2)}, u32[]{:S(2)}) async-start(bf16[16,128,256]{1,2,0:T(8,128)(2,1)} %copy.90), calls=%async_computation.3 | async-start | bytes 2097152 | tf_op jit(solution)/shard_map/all_to_all | solution.py:50
  274.6 77.5 %while.119 = (s32[]{:T(128)}, f32[512,1,128]{0,2,1:T(8,128)S(1)}, s32[64]{0:T(128)S(1)}, s32[]{:T(128)}, bf16[8192,128]{1,0:T(8,128)(2,1)}, /*index=5*/s32[512]{...) while((s32[]{:T(128)}, f32[512,1,128]{0,2,1:T(8,128)S(1)}, ...), condition=%wide.region_33.34_spmd, body=%wide.region_28.33_spmd.sunk | while | flops 203406336 | bytes 3296801 | solution.py:198
  291.1 2.8 conditional.10
  296.0 2.8 conditional.10
  300.8 2.8 conditional.10
  315.3 2.8 conditional.10
  349.3 2.8 conditional.10
  352.1 34.0 %all_gather.22 = f32[8192,2]{0,1:T(2,128)S(1)} all-gather(f32[512,2]{0,1:T(2,128)S(1)} %pad_maximum_fusion.4), channel_id=1, replica_groups=mesh['sec'=4,'ctx'=16,'tp'=4] {'ctx'}, dimensions={0}, use_global_device_ids=true | all-gather | bytes 69632 | tf_op jit(solution)/shard_map/all_gather | solution.py:22
  387.0 3.3 all-to-all-start.4
  391.9 2.9 all-to-all-done.4
  394.7 15.3 %all-gather = bf16[32,2,4,4,1,128]{5,0,4,2,1,3:T(8,128)(2,1)S(1)} all-gather(bf16[32,2,4,1,1,128]{5,0,4,2,1,3:T(8,128)(2,1)S(1)} %bitcast.266), channel_id=2, replica_groups=mesh['sec'=4,'ctx'=16,'tp'=4] {'tp'}, dimensions={3}, use_global_device_ids=true | all-gather | bytes 327680 | tf_op jit(solution)/shard_map/all_gather | solution.py:407
  411.2 4.5 fusion.167
  415.7 54.6 %while.120 = (s32[]{:T(128)}, f32[512,256]{0,1:T(8,128)S(1)}, s32[64]{0:T(128)S(1)}, s32[]{:T(128)}, bf16[8192,128]{1,0:T(8,128)(2,1)}, /*index=5*/s32[512]{0:T(...) while((s32[]{:T(128)}, f32[512,256]{0,1:T(8,128)S(1)}, ...), condition=%wide.region_40.41_spmd, body=%wide.region_35.40_spmd.sunk | while | flops 541620224 | bytes 9752105 | solution.py:386
  417.9 4.7 conditional.11
  424.7 4.7 conditional.11
  431.5 4.7 conditional.11
  438.3 4.7 conditional.11
  445.2 4.7 conditional.11
  452.0 4.7 conditional.11
  458.8 4.7 conditional.11
  465.6 4.7 conditional.11
  (478 shorter events, 307.9 us)
Async XLA Ops:
  7.2 57.7 %copy-start = (bf16[512,128]{1,0:T(8,128)(2,1)S(1)}, bf16[512,128]{1,0:T(8,128)(2,1)}, u32[]{:S(2)}) copy-start(bf16[512,128]{1,0:T(8,128)(2,1)} %param.38) | copy-start | bytes 393220
  7.2 113.5 %all-gather.4.cloned.1.call-start = ((), (), s32[]{:S(2)}) async-start(), calls=%async_computation.5 | async-start | bytes 4456448 | tf_op jit(solution)/shard_map/all_gather | solution.py:22
  10.7 9.3 %all-to-all-start.1 = ((bf16[32,4,128]{2,0,1:T(8,128)(2,1)}), bf16[32,4,128]{2,0,1:T(8,128)(2,1)S(1)}, u32[]{:S(2)}, u32[]{:S(2)}) async-start(bf16[32,4,128]{2,0,1:T(8,128)(2,1)} %bitcast.224), calls=%async_computation.1 | async-start | bytes 65536 | tf_op jit(solution)/shard_map/all_to_all | solution.py:297
  20.0 46.7 %all-to-all-start = ((bf16[32,4,128]{2,0,1:T(8,128)(2,1)}), bf16[32,4,128]{2,0,1:T(8,128)(2,1)S(1)}, u32[]{:S(2)}, u32[]{:S(2)}) async-start(bf16[32,4,128]{2,0,1:T(8,128)(2,1)} %bitcast.225), calls=%async_computation | async-start | bytes 65536 | tf_op jit(solution)/shard_map/all_to_all | solution.py:298
  105.8 19.3 %copy-start.3 = (s32[64]{0:T(128)S(1)}, s32[64]{0:T(128)}, u32[]{:S(2)}) copy-start(s32[64]{0:T(128)} %param.43) | copy-start | bytes 772
  127.2 1.4 copy-start.10
  127.2 2.0 copy-start.6
  131.8 1.4 copy-start.10
  131.8 2.0 copy-start.6
  136.5 1.4 copy-start.10
  136.5 2.0 copy-start.6
  141.1 1.4 copy-start.10
  141.1 2.0 copy-start.6
  145.8 1.4 copy-start.10
  145.8 2.0 copy-start.6
  150.4 1.4 copy-start.10
  150.4 2.0 copy-start.6
  155.1 1.4 copy-start.10
  155.1 2.0 copy-start.6
  159.7 1.4 copy-start.10
  159.7 2.0 copy-start.6
  234.6 12.7 %copy-start.2 = (bf16[8192,128]{1,0:T(8,128)(2,1)}, bf16[8192,128]{1,0:T(8,128)(2,1)S(1)}, u32[]{:S(2)}) copy-start(bf16[8192,128]{1,0:T(8,128)(2,1)S(1)} %get-tuple-element.2596) | copy-start | bytes 6291460
  237.1 22.9 %copy-start.9 = (f32[1,512]{1,0:T(1,128)S(1)}, f32[1,512]{1,0:T(1,128)}, u32[]{:S(2)}) copy-start(f32[1,512]{1,0:T(1,128)} %copy-done.8) | copy-start | bytes 6148
  239.3 14.2 %all-to-all-start.2 = ((f32[16,1,2048]{2,1,0:T(1,128)}), f32[16,1,2048]{2,1,0:T(1,128)}, u32[]{:S(2)}, u32[]{:S(2)}) async-start(f32[16,1,2048]{2,1,0:T(1,128)} %broadcast_in_dim.223), calls=%async_computation.2 | async-start | bytes 262144 | tf_op jit(solution)/shard_map/all_to_all | solution.py:27
  247.3 163.9 %all-gather.6.cloned.1.call-start = ((), (), s32[]{:S(2)}) async-start(), calls=%async_computation.6 | async-start | bytes 4456448 | tf_op jit(solution)/shard_map/all_gather | solution.py:22
  267.1 7.4 %copy-start.4 = (bf16[512,1,128]{2,0,1:T(8,128)(2,1)S(1)}, bf16[512,1,128]{2,0,1:T(8,128)(2,1)}, u32[]{:S(2)}) copy-start(bf16[512,1,128]{2,0,1:T(8,128)(2,1)} %get-tuple-element.2612) | copy-start | bytes 393220
  267.1 7.4 %copy-start.11 = (s32[512]{0:T(512)S(1)}, s32[512]{0:T(512)}, u32[]{:S(2)}) copy-start(s32[512]{0:T(512)} %get-tuple-element.2616) | copy-start | bytes 6148
  267.1 7.4 %copy-start.13 = (f32[1,512]{1,0:T(1,128)S(1)}, f32[1,512]{1,0:T(1,128)}, u32[]{:S(2)}) copy-start(f32[1,512]{1,0:T(1,128)} %copy-done.12) | copy-start | bytes 6148
  268.5 117.6 %all-to-all-start.3 = ((bf16[16,128,256]{1,2,0:T(8,128)(2,1)}), bf16[16,128,256]{1,2,0:T(8,128)(2,1)S(1)}, u32[]{:S(2)}, u32[]{:S(2)}) async-start(bf16[16,128,256]{1,2,0:T(8,128)(2,1)} %copy.90), calls=%async_computation.3 | async-start | bytes 2097152 | tf_op jit(solution)/shard_map/all_to_all | solution.py:50
  387.0 7.7 %all-to-all-start.4 = ((bf16[128,2,1,1,128]{4,1,3,2,0:T(2,128)(2,1)}), bf16[128,2,1,1,128]{4,1,3,2,0:T(2,128)(2,1)S(1)}, u32[]{:S(2)}, u32[]{:S(2)}) async-start(bf16[128,2,1,1,128]{4,1,3,2,0:T(2,128)(2,1)} %copy.91), calls=%async_computation.4 | async-start | bytes 131072 | tf_op jit(solution)/shard_map/all_to_all | solution.py:406
  411.2 4.6 copy-start.1
  411.2 4.6 copy-start.5
  (10 other events, 5.8 us)
Sparse Core Ops, SparseCore 0:
  10.6 110.0 all-gather.3
  258.2 104.5 all-gather.5
where the time goes:
time: 481 us; the launch traced here: 478 us
  matrix products  138 us (29%)
  blocking collectives  127 us (26%)
  loops' own time  64.9 us (13%)
  other arithmetic  55.2 us (11%)
  local copies, waits for them, and re-layouts  28 us (6%)
  starting transfers between devices  26 us (5%)
  waiting for transfers between devices  24.5 us (5%)
  between operations  14.4 us (3%)
    dot_general x38, matrix products, masked_scores(): jnp.einsum('qhd,khd->hqk', queries, key_block, preferred_element_type=jnp...  46.2 us
    all_gather x1, blocking collectives, per_device(): lax.all_gather(memory_keys, 'ctx', axis=0, tiled=True)  41.2 us
    dot_general x20, matrix products, attend_update(): jnp.einsum('hqk,khd->qhd', weights, value_block, preferred_element_type=j...  40.3 us
    all_gather x1, blocking collectives, per_device(): lax.all_gather(memory_values, 'ctx', axis=0, tiled=True)  36.3 us
    all_gather x1, blocking collectives, in_one_piece(): lax.all_gather(both, axis, axis=dim, tiled=True)  34 us
    reduce_min x41, other arithmetic, skipped(): return jnp.min(key_positions) > jnp.max(query_positions)  27 us
    dot_general x16, matrix products, query_update(): jnp.einsum('hqk,khd->qhd', score_grad, key_block, preferred_element_type=...  23.5 us
    another operation x1, loops' own time, query_grads(): lax.fori_loop(0, key_count // block_length, query_visit, jnp.zeros(querie...  20.8 us
  transfers between devices with their start and end apart: 7, of which 4 were waited for; matrix products, arithmetic and copies ran while one was open for 17% of the time, Pallas kernels for 0%

commit v1 on v0

v1 whole, which is shorter than its diff:
```python
import functools
import math

import jax
import jax.numpy as jnp
from jax import lax
from jax.experimental import pallas as pl
from jax.experimental.pallas import tpu as pltpu
from jax.sharding import PartitionSpec as P

HEAD_DIM = 128
EPS = 1e-06
NEG = -1e30
SCALE = 1.0 / math.sqrt(HEAD_DIM)
C2 = SCALE * math.log2(math.e)
TQ = 256
MESH = pl.DeviceIdType.MESH
F32 = jnp.float32
BF16 = jnp.bfloat16
SELF, CROSS = 0, 1


def dot(a, b, ca, cb):
    return lax.dot_general(a, b, (((ca,), (cb,)), ((), ())), preferred_element_type=F32)


def pack_rows(ref, vectors):
    row = 0
    for v in vectors:
        for i in range(v.shape[1] // 128):
            ref[row : row + 1, :] = v[:, i * 128 : (i + 1) * 128]
            row += 1


def unpack_rows(tile, row, count):
    return jnp.concatenate([tile[row + i : row + i + 1, :] for i in range(count)], axis=1)


def kernel(
    nz, nsec, ntp, n_sems,
    bs, q_in, k_in, v_in, sgain, sgrad, cq_in, mk_in, mv_in, cgain, cgrad,
    self_out, cross_out, query_grad, key_grad, value_grad, cross_query_grad, mkey_grad, mvalue_grad,
    kv, qs, mb, acc, ml, ot, lifted, osend, orecv, ostat, ostat_r, nsend, nrecv, do, dstat,
    dq, dqs, dqr, kacc, rs_s, rs_r, ms, mrs_s, mrs_r, mfin, mout,
    ssem, rsem, lsem,
):
    rows = q_in.shape[0]
    mrows = mk_in.shape[0]
    srows = nsec * mrows
    half = nz // 2
    full = nsec * ntp * HEAD_DIM
    nt = rows // TQ
    nsub = rows // 128

    sec, ctx, tp = lax.axis_index("sec"), lax.axis_index("ctx"), lax.axis_index("tp")
    z, x = ctx // 2, ctx % 2
    head = sec * ntp + tp

    def dev(zz, xx):
        return (sec, zz * 2 + xx, tp)

    right = dev(lax.rem(z + 1, nz), x)
    left = dev(lax.rem(z + nz - 1, nz), x)
    partner = dev(z, 1 - x)

    def peer(o):
        return (lax.rem(sec + o // ntp, nsec), ctx, lax.rem(tp + o % ntp, ntp))

    n_peers = nsec * ntp

    count = [0]

    def sem_id():
        count[0] += 1
        assert count[0] <= n_sems
        return count[0] - 1

    sent = []

    def copy(src, dst, i, to):
        return pltpu.make_async_remote_copy(
            src_ref=src, dst_ref=dst, send_sem=ssem.at[i], recv_sem=rsem.at[i], device_id=to, device_id_type=MESH
        )

    def send(src, dst, i, to):
        c = copy(src, dst, i, to)
        c.start()
        sent.append(c)

    def arrive(dst, i, frm):
        copy(dst, dst, i, frm).wait_recv()

    local = [
        pltpu.make_async_copy(k_in, kv.at[z, 0], lsem.at[0]),
        pltpu.make_async_copy(v_in, kv.at[z, 1], lsem.at[1]),
        pltpu.make_async_copy(q_in, qs.at[SELF, x], lsem.at[2]),
        pltpu.make_async_copy(cq_in, qs.at[CROSS, x], lsem.at[3]),
    ]
    own_cols = pl.ds(pl.multiple_of(head * HEAD_DIM, HEAD_DIM), HEAD_DIM)
    own_rows = pl.ds(pl.multiple_of(sec * mrows, mrows), mrows)
    local += [
        pltpu.make_async_copy(mk_in.at[:, own_cols], mb.at[z, 0, own_rows, :], lsem.at[4]),
        pltpu.make_async_copy(mv_in.at[:, own_cols], mb.at[z, 1, own_rows, :], lsem.at[5]),
    ]
    for c in local:
        c.start()

    barrier = pltpu.get_barrier_semaphore()
    everyone = [right, left, partner] + [peer(o) for o in range(1, n_peers)]
    for to in everyone:
        pl.semaphore_signal(barrier, inc=1, device_id=to, device_id_type=MESH)
    pl.semaphore_wait(barrier, len(everyone))

    mem_ids = []
    for o in range(1, nsec):
        to = (lax.rem(sec + o, nsec), ctx, tp)
        cols = pl.ds(pl.multiple_of((lax.rem(sec + o, nsec) * ntp + tp) * HEAD_DIM, HEAD_DIM), HEAD_DIM)
        for j, src in enumerate((mk_in, mv_in)):
            i = sem_id()
            send(src.at[:, cols], mb.at[z, j, own_rows, :], i, to)
            mem_ids.append((o, j, i))

    def zoff(d):
        return lax.rem(z + nz + d, nz)

    def ring_ids():
        return [(sem_id(), sem_id()) for _ in range(half)]

    kv_ids, mb_ids = ring_ids(), ring_ids()

    def ring_send(buf, ids, s):
        r, l = ids[s - 1]
        a, b = zoff(-(s - 1)), zoff(s - 1)
        if s < half:
            send(buf.at[a], buf.at[a], r, right)
            send(buf.at[b], buf.at[b], l, left)
        else:
            send(buf.at[a, 0], buf.at[a, 0], r, right)
            send(buf.at[b, 1], buf.at[b, 1], l, left)

    def ring_arrive(buf, ids, s):
        r, l = ids[s - 1]
        a, b = zoff(-s), zoff(s)
        if s < half:
            arrive(buf.at[a], r, left)
            arrive(buf.at[b], l, right)
        else:
            arrive(buf.at[a, 0], r, left)
            arrive(buf.at[b, 1], l, right)

    local[0].wait()
    local[1].wait()
    ring_send(kv, kv_ids, 1)
    q_ids = [sem_id(), sem_id()]
    for a in (SELF, CROSS):
        local[2 + a].wait()
        send(qs.at[a, x], qs.at[a, x], q_ids[a], partner)

    acc[...] = jnp.zeros_like(acc)
    dq[...] = jnp.zeros_like(dq)
    for a in (SELF, CROSS):
        for h in range(2):
            ml[a, h, 0:1, :] = jnp.full((1, rows), NEG, F32)
            ml[a, h, 1:2, :] = jnp.zeros((1, rows), F32)
    for a, (gain, grad) in enumerate(((sgain, sgrad), (cgain, cgrad))):
        lifted[a] = (gain[...] * grad[...].astype(F32)).T

    def query_positions(h, t):
        lane = lax.broadcasted_iota(jnp.int32, (1, 128), 1)
        first = (z * 2 + h) * nsub + t * (TQ // 128)
        return jnp.concatenate([bs[first + i] * 128 + lane for i in range(TQ // 128)], axis=1)

    def masked(s, slot, h, t):
        qpos = query_positions(h, t)
        first = (slot * 2 + x) * nsub
        row = lax.broadcasted_iota(jnp.int32, (128, TQ), 0)
        out = []
        for kb in range(nsub):
            gone = row > qpos - bs[first + kb] * 128
            out.append(jnp.where(gone, NEG, s[kb * 128 : (kb + 1) * 128, :]))
        return jnp.concatenate(out, axis=0)

    def forward(a, h, keys, values_t, slot):
        for t in range(nt):
            cols = slice(t * TQ, (t + 1) * TQ)
            s = dot(keys, qs[a, h, cols, :], 1, 1)
            if slot is not None:
                s = masked(s, slot, h, t)
            old = ml[a, h, 0:1, cols]
            new = jnp.maximum(old, jnp.max(s, axis=0, keepdims=True))
            p = jnp.exp2((s - new) * C2)
            shrink = jnp.exp2((old - new) * C2)
            ml[a, h, 0:1, cols] = new
            ml[a, h, 1:2, cols] = ml[a, h, 1:2, cols] * shrink + jnp.sum(p, axis=0, keepdims=True)
            acc[a, h, :, cols] = acc[a, h, :, cols] * shrink + dot(values_t, p.astype(BF16), 1, 0)

    def self_forward(slot, h):
        forward(SELF, h, kv[slot, 0], kv[slot, 1].T, slot)

    def cross_group(g, j):
        per = rows // srows
        return mb[pl.ds(g * per, per), j].reshape(rows, HEAD_DIM)

    n_groups = nz * srows // rows

    def cross_forward():
        def one(i, c):
            g, h = i // 2, i % 2
            forward(CROSS, h, cross_group(g, 0), cross_group(g, 1).T, None)
            return c

        lax.fori_loop(0, n_groups * 2, one, 0)

    self_forward(z, x)
    local[4].wait()
    local[5].wait()
    for o, j, i in mem_ids:
        frm = lax.rem(sec + nsec - o, nsec)
        dst = mb.at[z, j, pl.ds(pl.multiple_of(frm * mrows, mrows), mrows), :]
        arrive(dst, i, (frm, ctx, tp))
    ring_send(mb, mb_ids, 1)
    for a in (SELF, CROSS):
        arrive(qs.at[a, 1 - x], q_ids[a], partner)
    self_forward(z, 1 - x)
    for s in range(1, half):
        ring_arrive(kv, kv_ids, s)
        ring_send(kv, kv_ids, s + 1)
        ring_arrive(mb, mb_ids, s)
        ring_send(mb, mb_ids, s + 1)

        def pair(i, c, s=s):
            self_forward(zoff((2 * (i // 2) - 1) * s), i % 2)
            return c

        lax.fori_loop(0, 4, pair, 0)
    ring_arrive(kv, kv_ids, half)
    ring_arrive(mb, mb_ids, half)

    def last(i, c):
        self_forward(zoff(half), i)
        return c

    lax.fori_loop(0, 2, last, 0)

    o_ids = [(sem_id(), sem_id()) for _ in range(2)]
    n_ids = [[sem_id() for _ in range(1, n_peers)] for _ in range(2)]
    do_ids = [(sem_id(), sem_id()) for _ in range(2)]
    dq_ids = [sem_id(), sem_id()]

    def normed(a, h):
        total = ml[a, h, 1:2, :]
        return acc[a, h] * (1.0 / total), ml[a, h, 0:1, :] * C2 + jnp.log2(total)

    def send_partial(a):
        o, lse = normed(a, 1 - x)
        osend[a] = o.astype(BF16)
        pack_rows(ostat.at[a], [lse])
        send(osend.at[a], orecv.at[a], o_ids[a][0], partner)
        send(ostat.at[a], ostat_r.at[a], o_ids[a][1], partner)

    def combine(a):
        o0, l0 = normed(a, x)
        arrive(orecv.at[a], o_ids[a][0], partner)
        arrive(ostat_r.at[a], o_ids[a][1], partner)
        l1 = unpack_rows(ostat_r[a], 0, nsub)
        top = jnp.maximum(l0, l1)
        w0, w1 = jnp.exp2(l0 - top), jnp.exp2(l1 - top)
        total = w0 + w1
        inv = 1.0 / total
        o = o0 * (w0 * inv) + orecv[a].astype(F32) * (w1 * inv)
        ot[a] = o
        lse = top + jnp.log2(total)
        pack_rows(dstat.at[a, x], [lse])
        pack_rows(
            nsend.at[a],
            [jnp.sum(o * o, axis=0, keepdims=True), jnp.sum(lifted[a] * o, axis=0, keepdims=True)],
        )
        for k in range(1, n_peers):
            send(nsend.at[a], nrecv.at[a, k - 1], n_ids[a][k - 1], peer(k))

    def norm(a, gain, out):
        total = nsend[a]
        for k in range(1, n_peers):
            o = n_peers - k
            frm = (lax.rem(sec + nsec - k // ntp, nsec), ctx, lax.rem(tp + ntp - k % ntp, ntp))
            arrive(nrecv.at[a, k - 1], n_ids[a][k - 1], frm)
            total = total + nrecv[a, k - 1]
        scale = lax.rsqrt(unpack_rows(total, 0, nsub) / full + EPS)
        slope = unpack_rows(total, nsub, nsub) / full
        o = ot[a]
        g = (scale * (lifted[a] - o * (scale * scale * slope))).astype(BF16)
        do[a, x] = g
        delta = jnp.sum(g.astype(F32) * o, axis=0, keepdims=True)
        pack_rows(dstat.at[a, x, nsub : 2 * nsub], [delta])
        send(do.at[a, x], do.at[a, x], do_ids[a][0], partner)
        send(dstat.at[a, x], dstat.at[a, x], do_ids[a][1], partner)
        out[...] = (gain[...] * (o * scale).T).astype(BF16)

    send_partial(SELF)
    cross_forward()
    send_partial(CROSS)
    combine(SELF)
    combine(CROSS)
    norm(SELF, sgain, self_out)
    norm(CROSS, cgain, cross_out)

    def backward(a, h, keys, values, keys_t, slot, into):
        dk = dv = None
        for t in range(nt):
            cols = slice(t * TQ, (t + 1) * TQ)
            q = qs[a, h, cols, :]
            g = do[a, h, :, cols]
            stat = dstat[a, h]
            lse = unpack_rows(stat, t * (TQ // 128), TQ // 128)
            delta = unpack_rows(stat, nsub + t * (TQ // 128), TQ // 128)
            s = dot(keys, q, 1, 1)
            if slot is not None:
                s = masked(s, slot, h, t)
            p = jnp.exp2(s * C2 - lse)
            ds = (p * (dot(values, g, 1, 0) - delta)).astype(BF16)
            dv_t = dot(p.astype(BF16), g, 1, 1)
            dk_t = dot(ds, q, 1, 0)
            dv = dv_t if dv is None else dv + dv_t
            dk = dk_t if dk is None else dk + dk_t
            dq[a, h, :, cols] = dq[a, h, :, cols] + dot(keys_t, ds, 1, 0)
        kacc[into, 0] = kacc[into, 0] + dk * SCALE
        kacc[into, 1] = kacc[into, 1] + dv

    def self_backward(slot, h, into):
        backward(SELF, h, kv[slot, 0], kv[slot, 1], kv[slot, 0].T, slot, into)

    rs_ids = ring_ids()
    mrs_ids = ring_ids()

    def reduce_step(s, part, recv, snd, ids):
        r, l = ids[s - 1]
        if s == 1:
            snd[0, 0, 0] = part(0, 0).astype(BF16)
            snd[1, 0, 1] = part(1, 1).astype(BF16)
            send(snd.at[0, 0, 0], recv.at[0, 0, 0], r, right)
            send(snd.at[1, 0, 1], recv.at[1, 0, 1], l, left)
            return
        reduce_arrive(s - 1, recv, ids)
        for d in range(2):
            for j in range(2):
                own = part(d, j)
                if s > 2 or j == d:
                    own = own + recv[d, s - 2, j].astype(F32)
                snd[d, s - 1, j] = own.astype(BF16)
        send(snd.at[0, s - 1], recv.at[0, s - 1], r, right)
        send(snd.at[1, s - 1], recv.at[1, s - 1], l, left)

    def reduce_arrive(s, recv, ids):
        r, l = ids[s - 1]
        if s == 1:
            arrive(recv.at[0, 0, 0], r, left)
            arrive(recv.at[1, 0, 1], l, right)
        else:
            arrive(recv.at[0, s - 1], r, left)
            arrive(recv.at[1, s - 1], l, right)

    def do_arrive(a):
        arrive(do.at[a, 1 - x], do_ids[a][0], partner)
        arrive(dstat.at[a, 1 - x], do_ids[a][1], partner)

    def cross_backward():
        per = rows // srows

        def one(g, c):
            kacc[0] = jnp.zeros_like(kacc[0])
            keys, values = cross_group(g, 0), cross_group(g, 1)
            keys_t = keys.T

            def each(h, c2):
                backward(CROSS, h, cross_group(g, 0), cross_group(g, 1), keys_t, None, 0)
                return c2

            lax.fori_loop(0, 2, each, 0)
            for j in range(2):
                ms[pl.ds(g * per, per), j] = kacc[0, j].reshape(per, srows, HEAD_DIM)
            return c

        lax.fori_loop(0, n_groups, one, 0)

    def mem_part(s):
        return lambda d, j: ms[zoff((1 - 2 * d) * (half + 1 - s)), j]

    kacc[0] = jnp.zeros_like(kacc[0])
    self_backward(zoff(half), x, 0)
    do_arrive(SELF)
    self_backward(zoff(half), 1 - x, 0)
    reduce_step(1, lambda d, j: kacc[0, j], rs_r, rs_s, rs_ids)
    for s in range(2, half + 1):
        dist = half + 1 - s
        kacc[...] = jnp.zeros_like(kacc)

        def back_pair(i, c, dist=dist):
            d, h = i // 2, i % 2
            self_backward(zoff((1 - 2 * d) * dist), h, d)
            return c

        lax.fori_loop(0, 4, back_pair, 0)
        reduce_step(s, lambda d, j: kacc[d, j], rs_r, rs_s, rs_ids)
        if s == 2:
            do_arrive(CROSS)
            cross_backward()
            dqs[CROSS] = dq[CROSS, 1 - x].astype(BF16)
            send(dqs.at[CROSS], dqr.at[CROSS], dq_ids[CROSS], partner)
            reduce_step(1, mem_part(1), mrs_r, mrs_s, mrs_ids)
        else:
            reduce_step(s - 1, mem_part(s - 1), mrs_r, mrs_s, mrs_ids)
    kacc[0] = jnp.zeros_like(kacc[0])

    def back_own(h, c):
        self_backward(z, h, 0)
        return c

    lax.fori_loop(0, 2, back_own, 0)
    dqs[SELF] = dq[SELF, 1 - x].astype(BF16)
    send(dqs.at[SELF], dqr.at[SELF], dq_ids[SELF], partner)
    reduce_step(half, mem_part(half), mrs_r, mrs_s, mrs_ids)

    def reduced(own, recv, j):
        return (own + recv[0, half - 1, j].astype(F32) + recv[1, half - 1, j].astype(F32)).astype(BF16)

    def finish_query(a, out):
        arrive(dqr.at[a], dq_ids[a], partner)
        out[...] = ((dq[a, x] + dqr[a].astype(F32)) * SCALE).T.astype(BF16)

    finish_query(CROSS, cross_query_grad)
    reduce_arrive(half, rs_r, rs_ids)
    key_grad[...] = reduced(kacc[0, 0], rs_r, 0)
    value_grad[...] = reduced(kacc[0, 1], rs_r, 1)
    reduce_arrive(half, mrs_r, mrs_ids)
    for j in range(2):
        mfin[j] = reduced(ms[z, j], mrs_r, j)
    ret_ids = [sem_id() for _ in range(1, n_peers)]
    for k in range(1, n_peers):
        to = peer(k)
        src_rows = pl.ds(pl.multiple_of(to[0] * mrows, mrows), mrows)
        send(mfin.at[:, src_rows, :], mout.at[:, :, own_cols], ret_ids[k - 1], to)
    mine = pltpu.make_async_copy(mfin.at[:, own_rows, :], mout.at[:, :, own_cols], lsem.at[0])
    mine.start()
    finish_query(SELF, query_grad)
    mine.wait()
    for k in range(1, n_peers):
        fs, ft = lax.rem(sec + nsec - k // ntp, nsec), lax.rem(tp + ntp - k % ntp, ntp)
        cols = pl.ds(pl.multiple_of((fs * ntp + ft) * HEAD_DIM, HEAD_DIM), HEAD_DIM)
        arrive(mout.at[:, :, cols], ret_ids[k - 1], (fs, ctx, ft))
    mkey_grad[...] = mout[0]
    mvalue_grad[...] = mout[1]
    for c in sent:
        c.wait_send()


def per_device(nz, nsec, ntp, *args):
    (sq, sk, sv, sgain, sgrad, cq, mk, mv, cgain, cgrad, bs) = args
    rows = sq.shape[0]
    mrows = mk.shape[0]
    half = nz // 2
    srows = nsec * mrows
    n_sems = 160
    any_spec = pl.BlockSpec(memory_space=pl.ANY)
    vmem = pl.BlockSpec(memory_space=pltpu.VMEM)
    smem = pl.BlockSpec(memory_space=pltpu.SMEM)
    frame = jax.ShapeDtypeStruct((rows, HEAD_DIM), BF16)
    memory = jax.ShapeDtypeStruct(mk.shape, BF16)
    V = pltpu.VMEM
    return pl.pallas_call(
        functools.partial(kernel, nz, nsec, ntp, n_sems),
        out_shape=(frame, frame, frame, frame, frame, frame, memory, memory),
        in_specs=[smem, any_spec, any_spec, any_spec, vmem, vmem, any_spec, any_spec, any_spec, vmem, vmem],
        out_specs=(vmem,) * 8,
        scratch_shapes=[
            V((nz, 2, rows, HEAD_DIM), BF16),
            V((2, 2, rows, HEAD_DIM), BF16),
            V((nz, 2, srows, HEAD_DIM), BF16),
            V((2, 2, HEAD_DIM, rows), F32),
            V((2, 2, 8, rows), F32),
            V((2, HEAD_DIM, rows), F32),
            V((2, HEAD_DIM, rows), F32),
            V((2, HEAD_DIM, rows), BF16),
            V((2, HEAD_DIM, rows), BF16),
            V((2, 8, 128), F32),
            V((2, 8, 128), F32),
            V((2, 8, 128), F32),
            V((2, nsec * ntp, 8, 128), F32),
            V((2, 2, HEAD_DIM, rows), BF16),
            V((2, 2, 8, 128), F32),
            V((2, 2, HEAD_DIM, rows), F32),
            V((2, HEAD_DIM, rows), BF16),
            V((2, HEAD_DIM, rows), BF16),
            V((2, 2, rows, HEAD_DIM), F32),
            V((2, half, 2, rows, HEAD_DIM), BF16),
            V((2, half, 2, rows, HEAD_DIM), BF16),
            V((nz, 2, srows, HEAD_DIM), F32),
            V((2, half, 2, srows, HEAD_DIM), BF16),
            V((2, half, 2, srows, HEAD_DIM), BF16),
            V((2, srows, HEAD_DIM), BF16),
            V((2, mrows, nsec * ntp * HEAD_DIM), BF16),
            pltpu.SemaphoreType.DMA((n_sems,)),
            pltpu.SemaphoreType.DMA((n_sems,)),
            pltpu.SemaphoreType.DMA((8,)),
        ],
        compiler_params=pltpu.CompilerParams(
            collective_id=0, has_side_effects=True, vmem_limit_bytes=48 * 1024 * 1024
        ),
        cost_estimate=pl.CostEstimate(flops=9_000_000_000, bytes_accessed=4_000_000, transcendentals=10_000_000),
    )(bs, sq, sk, sv, sgain.reshape(1, -1), sgrad, cq, mk, mv, cgain.reshape(1, -1), cgrad)


def solution(mesh):
    nz, nsec, ntp = mesh.shape["ctx"] // 2, mesh.shape["sec"], mesh.shape["tp"]
    heads = ("sec", "tp")
    frame, gain, memory = P("ctx", heads), P(heads), P(("sec", "ctx"), None)
    return jax.shard_map(
        functools.partial(per_device, nz, nsec, ntp),
        mesh=mesh,
        in_specs=(frame, frame, frame, gain, frame, frame, memory, memory, gain, frame, P()),
        out_specs=(frame,) * 6 + (memory,) * 2,
        check_vma=False,
    )
```

time: 481 us -> 114 us (0.24)
  matrix products: 138 us -> 0 us
  blocking collectives: 127 us -> 0 us
  Pallas kernels: 0 us -> 100 us
  loops' own time: 64.9 us -> 0 us
  other arithmetic: 55.2 us -> 0 us
  starting transfers between devices: 26 us -> 0 us
  waiting for transfers between devices: 24.5 us -> 0 us
  local copies, waits for them, and re-layouts: 28 us -> 13.1 us
  between operations: 14.4 us -> 0.68 us
    dot_general x106 -> x0, matrix products: 138 us -> none  [the longest x38 46.2 us: masked_scores(): jnp.einsum('qhd,khd->hqk', queries, key_block, preferred_element_type=jnp...]
    all_gather x4 -> x0, blocking collectives: 127 us -> none  [the longest x1 41.2 us: per_device(): lax.all_gather(memory_keys, 'ctx', axis=0, tiled=True)]
    pallas_call x0 -> x1, Pallas kernels: none -> 100 us  [per_device(): pl.pallas_call(functools.partial(kernel, nz, nsec, ntp, n_sems), out_shap...]
    another operation x55 -> x0, loops' own time: 64.9 us -> none  [the longest x1 20.8 us: query_grads(): lax.fori_loop(0, key_count // block_length, query_visit, jnp.zeros(querie...]
    reduce_min x41 -> x0, other arithmetic: 27 us -> none  [skipped(): return jnp.min(key_positions) > jnp.max(query_positions)]
    all_to_all x5 -> x0, starting transfers between devices: 26 us -> none  [the longest x1 7.98 us: sent_to_all(): return lax.all_to_all(copies, axis, split_axis=0, concat_axis=0, tiled=True)]
    reduce_sum x64 -> x0, other arithmetic: 17 us -> none  [the longest x49 5.53 us: frame_positions(): starts = jnp.sum(jnp.where(lookup, block_start[None, :], 0), axis=1)]
    all_gather x2 -> x0, waiting for transfers between devices: 14.9 us -> none  [in_one_piece(): lax.all_gather(both, axis, axis=dim, tiled=True)]
  transfers between devices with their start and end apart: 7 -> 0, of which waited for: 4 -> 0; matrix products, arithmetic and copies ran while one was open for 17% -> 0% of each run, Pallas kernels for 0% -> 0%
where the time goes in v1:
time: 114 us
  Pallas kernels  100 us (88%)
  local copies, waits for them, and re-layouts  13.1 us (11%)
    pallas_call x1, Pallas kernels, per_device(): pl.pallas_call(functools.partial(kernel, nz, nsec, ntp, n_sems), out_shap...  100 us
    unnamed x30, local copies, waits for them, and re-layouts  13.1 us

profile of v1, /device:TPU:1, one launch (start us, length us, event | category | flops | bytes accessed | tf_op | source)
XLA Modules:
  0.0 114.1 jit_solution(12210183957578881312)
XLA Ops:
  0.6 0.0 copy-start.8
  0.6 0.0 copy-start.9
  0.7 0.0 copy-start.10
  0.7 0.6 copy-done.8
  1.3 0.0 copy-done.9
  1.3 0.0 copy-done.10
  1.3 0.0 copy-start
  1.3 0.9 copy-done
  2.2 0.0 copy-start.1
  2.2 0.9 copy-done.1
  3.1 0.0 copy-start.2
  3.1 0.9 copy-done.2
  4.0 0.0 copy-start.3
  4.0 0.9 copy-done.3
  4.9 0.0 copy-start.4
  4.9 0.9 copy-done.4
  5.8 0.0 copy-start.5
  5.9 0.9 copy-done.5
  6.8 0.0 copy-start.6
  6.8 0.9 copy-done.6
  7.7 0.0 copy-start.7
  7.7 0.9 copy-done.7
  8.6 100.3 %shard_map.170 = (bf16[512,128]{1,0:T(8,128)(2,1)S(1)}, bf16[512,128]{1,0:T(8,128)(2,1)S(1)}, bf16[512,128]{1,0:T(8,128)(2,1)S(1)}, bf16[512,128]{1,0:T(8,128)(2...) custom-call(s32[64]{0:T(128)S(1)} %copy-done.8, ...), custom_call_target="tpu_custom_call" | custom-call | flops 8999999488 | bytes 4000000 | tf_op jit(solution)/shard_map/pallas_call | solution.py:469
  108.8 0.7 copy.27
  109.5 0.7 copy.28
  110.2 0.7 copy.29
  110.8 0.7 copy.30
  111.5 0.7 copy.31
  112.1 0.7 copy.32
  112.8 0.7 copy.33
  113.4 0.7 copy.34
Async XLA Ops:
  0.6 0.7 copy-start.8
  0.6 0.7 copy-start.9
  0.7 0.7 copy-start.10
  1.3 0.9 copy-start
  2.2 0.9 copy-start.1
  3.1 0.9 copy-start.2
  4.0 0.9 copy-start.3
  4.9 0.9 copy-start.4
  5.8 0.9 copy-start.5
  6.8 0.9 copy-start.6
  7.7 0.9 copy-start.7

commit v2 on v1

v2 whole, which is shorter than its diff:
```python
import functools
import math

import jax
import jax.numpy as jnp
from jax import lax
from jax.experimental import pallas as pl
from jax.experimental.pallas import tpu as pltpu
from jax.sharding import PartitionSpec as P

HEAD_DIM = 128
EPS = 1e-06
NEG = -1e30
SCALE = 1.0 / math.sqrt(HEAD_DIM)
C2 = SCALE * math.log2(math.e)
TQ = 256
MESH = pl.DeviceIdType.MESH
F32 = jnp.float32
BF16 = jnp.bfloat16
SELF, CROSS = 0, 1


def dot(a, b, ca, cb):
    return lax.dot_general(a, b, (((ca,), (cb,)), ((), ())), preferred_element_type=F32)


def pack_rows(ref, vectors):
    row = 0
    for v in vectors:
        for i in range(v.shape[1] // 128):
            ref[row : row + 1, :] = v[:, i * 128 : (i + 1) * 128]
            row += 1


def unpack_rows(tile, row, count):
    return jnp.concatenate([tile[row + i : row + i + 1, :] for i in range(count)], axis=1)


def kernel(
    nz, nsec, ntp, n_sems,
    bs, q_in, k_in, v_in, sgain, sgrad, cq_in, mk_in, mv_in, cgain, cgrad,
    self_out, cross_out, query_grad, key_grad, value_grad, cross_query_grad, mkey_grad, mvalue_grad,
    kv, qs, mb, acc, ml, ot, lifted, osend, orecv, ostat, ostat_r, nsend, nrecv, do, dstat,
    dq, dqs, dqr, kacc, rs_s, rs_r, ms, mrs_s, mrs_r, mfin, mout,
    grads, gains,
    ssem, rsem, lsem,
):
    rows = q_in.shape[0]
    mrows = mk_in.shape[0]
    srows = nsec * mrows
    half = nz // 2
    full = nsec * ntp * HEAD_DIM
    nsub = rows // 128

    sec, ctx, tp = lax.axis_index("sec"), lax.axis_index("ctx"), lax.axis_index("tp")
    z, x = ctx // 2, ctx % 2
    head = sec * ntp + tp

    def dev(zz, xx):
        return (sec, zz * 2 + xx, tp)

    right = dev(lax.rem(z + 1, nz), x)
    left = dev(lax.rem(z + nz - 1, nz), x)
    partner = dev(z, 1 - x)

    def peer(o):
        return (lax.rem(sec + o // ntp, nsec), ctx, lax.rem(tp + o % ntp, ntp))

    n_peers = nsec * ntp

    count = [0]

    def sem_id():
        count[0] += 1
        assert count[0] <= n_sems
        return count[0] - 1

    sent = []

    def copy(src, dst, i, to):
        return pltpu.make_async_remote_copy(
            src_ref=src, dst_ref=dst, send_sem=ssem.at[i], recv_sem=rsem.at[i], device_id=to, device_id_type=MESH
        )

    def send(src, dst, i, to):
        c = copy(src, dst, i, to)
        c.start()
        sent.append(c)

    def arrive(dst, i, frm):
        copy(dst, dst, i, frm).wait_recv()

    own_cols = pl.ds(pl.multiple_of(head * HEAD_DIM, HEAD_DIM), HEAD_DIM)
    own_rows = pl.ds(pl.multiple_of(sec * mrows, mrows), mrows)
    local = [
        pltpu.make_async_copy(src, dst, lsem.at[i])
        for i, (src, dst) in enumerate(
            (
                (k_in, kv.at[z, 0]),
                (v_in, kv.at[z, 1]),
                (q_in, qs.at[SELF, x]),
                (cq_in, qs.at[CROSS, x]),
                (mk_in.at[:, own_cols], mb.at[z, 0, own_rows, :]),
                (mv_in.at[:, own_cols], mb.at[z, 1, own_rows, :]),
                (sgrad, grads.at[SELF]),
                (cgrad, grads.at[CROSS]),
                (sgain, gains.at[SELF]),
                (cgain, gains.at[CROSS]),
            )
        )
    ]
    for c in local:
        c.start()

    barrier = pltpu.get_barrier_semaphore()
    everyone = [right, left, partner] + [peer(o) for o in range(1, n_peers)]
    for to in everyone:
        pl.semaphore_signal(barrier, inc=1, device_id=to, device_id_type=MESH)
    pl.semaphore_wait(barrier, len(everyone))

    def zoff(d):
        return lax.rem(z + nz + d, nz)

    EARLY, LATE = ((0, 0), (1, 1)), ((0, 1), (1, 0))
    neighbour = (right, left)

    def ring_ids():
        return {(s, d, j): sem_id() for s in range(1, half + 1) for d in range(2) for j in range(2) if s < half or d == j}

    def towards(d, s):
        return zoff(-s) if d == 0 else zoff(s)

    kv_ids, mb_ids = ring_ids(), ring_ids()

    def ring_send(buf, ids, s, pairs):
        for d, j in pairs:
            if (s, d, j) in ids:
                ref = buf.at[towards(d, s - 1), j]
                send(ref, ref, ids[s, d, j], neighbour[d])

    def ring_arrive(buf, ids, s, pairs):
        for d, j in pairs:
            if (s, d, j) in ids:
                arrive(buf.at[towards(d, s), j], ids[s, d, j], neighbour[1 - d])

    def ring_pass(buf, ids, s, pairs):
        for pair in pairs:
            ring_arrive(buf, ids, s, (pair,))
            ring_send(buf, ids, s + 1, (pair,))

    mem_ids = []
    for o in range(1, nsec):
        to = (lax.rem(sec + o, nsec), ctx, tp)
        cols = pl.ds(pl.multiple_of((lax.rem(sec + o, nsec) * ntp + tp) * HEAD_DIM, HEAD_DIM), HEAD_DIM)
        for j, src in enumerate((mk_in, mv_in)):
            i = sem_id()
            send(src.at[:, cols], mb.at[z, j, own_rows, :], i, to)
            mem_ids.append((o, j, i))
    for pairs in (EARLY, LATE):
        for d, j in pairs:
            send((k_in, v_in)[j], kv.at[z, j], kv_ids[1, d, j], neighbour[d])
    q_ids = [sem_id(), sem_id()]
    for a, src in enumerate((q_in, cq_in)):
        send(src, qs.at[a, x], q_ids[a], partner)

    acc[...] = jnp.zeros_like(acc)
    for a in (SELF, CROSS):
        for h in range(2):
            ml[a, h, 0:1, :] = jnp.full((1, rows), NEG, F32)
            ml[a, h, 1:2, :] = jnp.zeros((1, rows), F32)

    def query_positions(h, begin, width):
        lane = lax.broadcasted_iota(jnp.int32, (1, 128), 1)
        first = (z * 2 + h) * nsub + begin // 128
        return jnp.concatenate([bs[first + i] * 128 + lane for i in range(width // 128)], axis=1)

    def masked(s, slot, h, begin):
        width = s.shape[1]
        qpos = query_positions(h, begin, width)
        first = (slot * 2 + x) * nsub
        row = lax.broadcasted_iota(jnp.int32, (128, width), 0)
        out = []
        for kb in range(nsub):
            gone = row > qpos - bs[first + kb] * 128
            out.append(jnp.where(gone, NEG, s[kb * 128 : (kb + 1) * 128, :]))
        return jnp.concatenate(out, axis=0)

    def forward(a, h, keys, values_t, slot):
        s = dot(keys, qs[a, h], 1, 1)
        if slot is not None:
            s = masked(s, slot, h, 0)
        old = ml[a, h, 0:1, :]
        new = jnp.maximum(old, jnp.max(s, axis=0, keepdims=True))
        p = jnp.exp2((s - new) * C2)
        shrink = jnp.exp2((old - new) * C2)
        ml[a, h, 0:1, :] = new
        ml[a, h, 1:2, :] = ml[a, h, 1:2, :] * shrink + jnp.sum(p, axis=0, keepdims=True)
        acc[a, h] = acc[a, h] * shrink + dot(values_t, p.astype(BF16), 1, 0)

    def self_forward(slot, h):
        forward(SELF, h, kv[slot, 0], kv[slot, 1].T, slot)

    def both_halves(slot):
        def one(h, c):
            self_forward(slot, h)
            return c

        lax.fori_loop(0, 2, one, 0)

    per = rows // srows
    n_groups = nz // per

    def cross_group(g, j):
        return jnp.concatenate([mb[zoff(g * per - 1 + i), j] for i in range(per)], axis=0)

    def cross_forward(g):
        def one(h, c):
            forward(CROSS, h, cross_group(g, 0), cross_group(g, 1).T, None)
            return c

        lax.fori_loop(0, 2, one, 0)

    for c in local[:3]:
        c.wait()
    self_forward(z, x)
    for c in local[3:]:
        c.wait()
    for o, j, i in mem_ids:
        frm = lax.rem(sec + nsec - o, nsec)
        dst = mb.at[z, j, pl.ds(pl.multiple_of(frm * mrows, mrows), mrows), :]
        arrive(dst, i, (frm, ctx, tp))
    ring_send(mb, mb_ids, 1, EARLY + LATE)
    arrive(qs.at[SELF, 1 - x], q_ids[SELF], partner)
    for s in range(1, half):
        ring_pass(kv, kv_ids, s, EARLY)
        if s == 1:
            self_forward(z, 1 - x)
        else:
            both_halves(zoff(1 - s))
        ring_pass(kv, kv_ids, s, LATE)
        if s > 1:
            both_halves(zoff(s - 1))
        ring_pass(mb, mb_ids, s, EARLY + LATE)
        if s == 1:
            dq[...] = jnp.zeros_like(dq)
            for a in (SELF, CROSS):
                lifted[a] = (gains[a] * grads[a].astype(F32)).T
    arrive(qs.at[CROSS, 1 - x], q_ids[CROSS], partner)
    cross_forward(0)
    both_halves(zoff(1 - half))
    both_halves(zoff(half - 1))
    ring_arrive(kv, kv_ids, half, EARLY)
    self_forward(zoff(half), 1 - x)

    o_ids = [(sem_id(), sem_id()) for _ in range(2)]
    n_ids = [[sem_id() for _ in range(1, n_peers)] for _ in range(2)]
    do_ids = [(sem_id(), sem_id()) for _ in range(2)]
    dq_ids = [sem_id(), sem_id()]

    def normed(a, h):
        total = ml[a, h, 1:2, :]
        return acc[a, h] * (1.0 / total), ml[a, h, 0:1, :] * C2 + jnp.log2(total)

    def send_partial(a):
        o, lse = normed(a, 1 - x)
        osend[a] = o.astype(BF16)
        pack_rows(ostat.at[a], [lse])
        send(osend.at[a], orecv.at[a], o_ids[a][0], partner)
        send(ostat.at[a], ostat_r.at[a], o_ids[a][1], partner)

    def combine(a):
        o0, l0 = normed(a, x)
        arrive(orecv.at[a], o_ids[a][0], partner)
        arrive(ostat_r.at[a], o_ids[a][1], partner)
        l1 = unpack_rows(ostat_r[a], 0, nsub)
        top = jnp.maximum(l0, l1)
        w0, w1 = jnp.exp2(l0 - top), jnp.exp2(l1 - top)
        total = w0 + w1
        inv = 1.0 / total
        o = o0 * (w0 * inv) + orecv[a].astype(F32) * (w1 * inv)
        ot[a] = o
        lse = top + jnp.log2(total)
        pack_rows(dstat.at[a, x], [lse])
        pack_rows(
            nsend.at[a],
            [jnp.sum(o * o, axis=0, keepdims=True), jnp.sum(lifted[a] * o, axis=0, keepdims=True)],
        )
        for k in range(1, n_peers):
            send(nsend.at[a], nrecv.at[a, k - 1], n_ids[a][k - 1], peer(k))

    def norm(a, out):
        total = nsend[a]
        for k in range(1, n_peers):
            frm = (lax.rem(sec + nsec - k // ntp, nsec), ctx, lax.rem(tp + ntp - k % ntp, ntp))
            arrive(nrecv.at[a, k - 1], n_ids[a][k - 1], frm)
            total = total + nrecv[a, k - 1]
        scale = lax.rsqrt(unpack_rows(total, 0, nsub) / full + EPS)
        slope = unpack_rows(total, nsub, nsub) / full
        o = ot[a]
        g = (scale * (lifted[a] - o * (scale * scale * slope))).astype(BF16)
        do[a, x] = g
        delta = jnp.sum(g.astype(F32) * o, axis=0, keepdims=True)
        pack_rows(dstat.at[a, x, nsub : 2 * nsub], [delta])
        send(do.at[a, x], do.at[a, x], do_ids[a][0], partner)
        send(dstat.at[a, x], dstat.at[a, x], do_ids[a][1], partner)
        out[...] = (gains[a] * (o * scale).T).astype(BF16)

    send_partial(SELF)
    self_forward(zoff(half), x)
    ring_arrive(mb, mb_ids, half, EARLY)
    for g in range(1, n_groups):
        cross_forward(g)
    send_partial(CROSS)
    combine(SELF)
    combine(CROSS)
    norm(SELF, self_out)

    def backward(a, h, keys, values, keys_t, slot, into):
        dk = dv = None
        for t in range(rows // TQ):
            cols = slice(t * TQ, (t + 1) * TQ)
            q = qs[a, h, cols, :]
            g = do[a, h, :, cols]
            stat = dstat[a, h]
            lse = unpack_rows(stat, t * (TQ // 128), TQ // 128)
            delta = unpack_rows(stat, nsub + t * (TQ // 128), TQ // 128)
            s = dot(keys, q, 1, 1)
            if slot is not None:
                s = masked(s, slot, h, t * TQ)
            p = jnp.exp2(s * C2 - lse)
            ds = (p * (dot(values, g, 1, 0) - delta)).astype(BF16)
            dv_t = dot(p.astype(BF16), g, 1, 1)
            dk_t = dot(ds, q, 1, 0)
            dv = dv_t if dv is None else dv + dv_t
            dk = dk_t if dk is None else dk + dk_t
            dq[a, h, :, cols] = dq[a, h, :, cols] + dot(keys_t, ds, 1, 0)
        kacc[into, 0] = kacc[into, 0] + dk * SCALE
        kacc[into, 1] = kacc[into, 1] + dv

    def self_backward(slot, h, into):
        backward(SELF, h, kv[slot, 0], kv[slot, 1], kv[slot, 0].T, slot, into)

    rs_ids, mrs_ids = ring_ids(), ring_ids()

    def reduce_step(dist, part, recv, snd, ids):
        for d, j in LATE + EARLY:
            if (dist, d, j) in ids:
                own = part(d, j)
                if (dist + 1, d, j) in ids:
                    arrive(recv.at[d, dist, j], ids[dist + 1, d, j], neighbour[1 - d])
                    own = own + recv[d, dist, j].astype(F32)
                snd[d, dist - 1, j] = own.astype(BF16)
                send(snd.at[d, dist - 1, j], recv.at[d, dist - 1, j], ids[dist, d, j], neighbour[d])

    def do_arrive(a):
        arrive(do.at[a, 1 - x], do_ids[a][0], partner)
        arrive(dstat.at[a, 1 - x], do_ids[a][1], partner)

    def cross_backward():
        def one(g, c):
            kacc[0] = jnp.zeros_like(kacc[0])
            keys_t = cross_group(g, 0).T

            def each(h, c2):
                backward(CROSS, h, cross_group(g, 0), cross_group(g, 1), keys_t, None, 0)
                return c2

            lax.fori_loop(0, 2, each, 0)
            for j in range(2):
                ms[pl.ds(g * per, per), j] = kacc[0, j].reshape(per, srows, HEAD_DIM)
            return c

        lax.fori_loop(0, n_groups, one, 0)

    def mem_own(dist, d, j):
        return ms[((dist if d == 0 else nz - dist) + 1) % nz, j]

    def mem_step(dist):
        reduce_step(dist, functools.partial(mem_own, dist), mrs_r, mrs_s, mrs_ids)

    def self_step(dist):
        reduce_step(dist, lambda d, j: kacc[0 if dist == half else 1 + d, j], rs_r, rs_s, rs_ids)

    def back_pair(dist, halves):
        def one(i, c):
            d, h = i // len(halves), i % len(halves)
            h = halves[0] if len(halves) == 1 else h
            self_backward(zoff((1 - 2 * d) * dist), h, 1 + d)
            return c

        lax.fori_loop(0, 2 * len(halves), one, 0)

    kacc[...] = jnp.zeros_like(kacc)
    self_backward(zoff(half), x, 0)
    norm(CROSS, cross_out)
    back_pair(half - 1, (x,))
    do_arrive(SELF)
    self_backward(zoff(half), 1 - x, 0)
    self_step(half)
    back_pair(half - 1, (1 - x,))
    self_step(half - 1)
    do_arrive(CROSS)
    cross_backward()
    mem_step(half)
    dqs[CROSS] = dq[CROSS, 1 - x].astype(BF16)
    send(dqs.at[CROSS], dqr.at[CROSS], dq_ids[CROSS], partner)
    for dist in range(half - 2, 0, -1):
        if dist == 1:
            kacc[0] = jnp.zeros_like(kacc[0])

            def back_own(h, c):
                self_backward(z, h, 0)
                return c

            lax.fori_loop(0, 2, back_own, 0)
            mem_step(2)
        kacc[1:3] = jnp.zeros_like(kacc[1:3])
        back_pair(dist, (0, 1))
        self_step(dist)
        if dist > 1:
            mem_step(dist + 1)
    dqs[SELF] = dq[SELF, 1 - x].astype(BF16)
    send(dqs.at[SELF], dqr.at[SELF], dq_ids[SELF], partner)
    mem_step(1)

    def reduced(own, recv, ids, j):
        for d in range(2):
            arrive(recv.at[d, 0, j], ids[1, d, j], neighbour[1 - d])
            own = own + recv[d, 0, j].astype(F32)
        return own.astype(BF16)

    def finish_query(a, out):
        arrive(dqr.at[a], dq_ids[a], partner)
        out[...] = ((dq[a, x] + dqr[a].astype(F32)) * SCALE).T.astype(BF16)

    finish_query(CROSS, cross_query_grad)
    for j in range(2):
        mfin[j] = reduced(ms[1, j], mrs_r, mrs_ids, j)
    ret_ids = [sem_id() for _ in range(1, n_peers)]
    for k in range(1, n_peers):
        to = peer(k)
        src_rows = pl.ds(pl.multiple_of(to[0] * mrows, mrows), mrows)
        send(mfin.at[:, src_rows, :], mout.at[:, :, own_cols], ret_ids[k - 1], to)
    mine = pltpu.make_async_copy(mfin.at[:, own_rows, :], mout.at[:, :, own_cols], lsem.at[0])
    mine.start()
    key_grad[...] = reduced(kacc[0, 0], rs_r, rs_ids, 0)
    value_grad[...] = reduced(kacc[0, 1], rs_r, rs_ids, 1)
    finish_query(SELF, query_grad)
    mine.wait()
    for k in range(1, n_peers):
        fs, ft = lax.rem(sec + nsec - k // ntp, nsec), lax.rem(tp + ntp - k % ntp, ntp)
        cols = pl.ds(pl.multiple_of((fs * ntp + ft) * HEAD_DIM, HEAD_DIM), HEAD_DIM)
        arrive(mout.at[:, :, cols], ret_ids[k - 1], (fs, ctx, ft))
    mkey_grad[...] = mout[0]
    mvalue_grad[...] = mout[1]
    for c in sent:
        c.wait_send()


def write_out(*refs):
    sems, stage = refs[-1], refs[16:24]
    ins = [pltpu.make_async_copy(refs[i], stage[i], sems.at[0, i]) for i in range(8)]
    outs = [pltpu.make_async_copy(stage[i], refs[8 + i], sems.at[1, i]) for i in range(8)]
    for c in ins:
        c.start()
    for c, d in zip(ins, outs):
        c.wait()
        d.start()
    for d in outs:
        d.wait()


def per_device(nz, nsec, ntp, *args):
    (sq, sk, sv, sgain, sgrad, cq, mk, mv, cgain, cgrad, bs) = args
    rows = sq.shape[0]
    mrows = mk.shape[0]
    half = nz // 2
    srows = nsec * mrows
    n_sems = 160
    hbm = pl.BlockSpec(memory_space=pltpu.HBM)
    vmem = pl.BlockSpec(memory_space=pltpu.VMEM)
    smem = pl.BlockSpec(memory_space=pltpu.SMEM)
    frame = jax.ShapeDtypeStruct((rows, HEAD_DIM), BF16)
    memory = jax.ShapeDtypeStruct(mk.shape, BF16)
    V = pltpu.VMEM
    results = pl.pallas_call(
        functools.partial(kernel, nz, nsec, ntp, n_sems),
        out_shape=(frame, frame, frame, frame, frame, frame, memory, memory),
        in_specs=[smem] + [hbm] * 10,
        out_specs=(vmem,) * 8,
        scratch_shapes=[
            V((nz, 2, rows, HEAD_DIM), BF16),
            V((2, 2, rows, HEAD_DIM), BF16),
            V((nz, 2, srows, HEAD_DIM), BF16),
            V((2, 2, HEAD_DIM, rows), F32),
            V((2, 2, 8, rows), F32),
            V((2, HEAD_DIM, rows), F32),
            V((2, HEAD_DIM, rows), F32),
            V((2, HEAD_DIM, rows), BF16),
            V((2, HEAD_DIM, rows), BF16),
            V((2, 8, 128), F32),
            V((2, 8, 128), F32),
            V((2, 8, 128), F32),
            V((2, nsec * ntp, 8, 128), F32),
            V((2, 2, HEAD_DIM, rows), BF16),
            V((2, 2, 8, 128), F32),
            V((2, 2, HEAD_DIM, rows), F32),
            V((2, HEAD_DIM, rows), BF16),
            V((2, HEAD_DIM, rows), BF16),
            V((3, 2, rows, HEAD_DIM), F32),
            V((2, half, 2, rows, HEAD_DIM), BF16),
            V((2, half, 2, rows, HEAD_DIM), BF16),
            V((nz, 2, srows, HEAD_DIM), F32),
            V((2, half, 2, srows, HEAD_DIM), BF16),
            V((2, half, 2, srows, HEAD_DIM), BF16),
            V((2, srows, HEAD_DIM), BF16),
            V((2, mrows, nsec * ntp * HEAD_DIM), BF16),
            V((2, rows, HEAD_DIM), BF16),
            V((2, 1, HEAD_DIM), F32),
            pltpu.SemaphoreType.DMA((n_sems,)),
            pltpu.SemaphoreType.DMA((n_sems,)),
            pltpu.SemaphoreType.DMA((10,)),
        ],
        compiler_params=pltpu.CompilerParams(
            collective_id=0, has_side_effects=True, vmem_limit_bytes=56 * 1024 * 1024
        ),
        cost_estimate=pl.CostEstimate(flops=9_000_000_000, bytes_accessed=4_000_000, transcendentals=10_000_000),
    )(bs, sq, sk, sv, sgain.reshape(1, -1), sgrad, cq, mk, mv, cgain.reshape(1, -1), cgrad)
    spec = pl.BlockSpec(memory_space=pl.ANY)
    return pl.pallas_call(
        write_out,
        out_shape=tuple(jax.ShapeDtypeStruct(r.shape, r.dtype) for r in results),
        in_specs=[spec] * 8,
        out_specs=(spec,) * 8,
        scratch_shapes=[V(r.shape, r.dtype) for r in results] + [pltpu.SemaphoreType.DMA((2, 8))],
        compiler_params=pltpu.CompilerParams(vmem_limit_bytes=56 * 1024 * 1024),
    )(*results)


def solution(mesh):
    nz, nsec, ntp = mesh.shape["ctx"] // 2, mesh.shape["sec"], mesh.shape["tp"]
    heads = ("sec", "tp")
    frame, gain, memory = P("ctx", heads), P(heads), P(("sec", "ctx"), None)
    return jax.shard_map(
        functools.partial(per_device, nz, nsec, ntp),
        mesh=mesh,
        in_specs=(frame, frame, frame, gain, frame, frame, memory, memory, gain, frame, P()),
        out_specs=(frame,) * 6 + (memory,) * 2,
        check_vma=False,
    )
```

time: 114 us -> 99 us (0.87)
  local copies, waits for them, and re-layouts: 13.1 us -> 0 us
  Pallas kernels: 100 us -> 98.1 us
    unnamed x30 -> x0, local copies, waits for them, and re-layouts: 13.1 us -> none
    pallas_call x1, Pallas kernels: 100 us -> 96 us  [per_device(): pl.pallas_call(functools.partial(kernel, nz, nsec, ntp, n_sems), out_shap...]
    pallas_call x0 -> x1, Pallas kernels: none -> 2.09 us  [per_device(): pl.pallas_call(write_out, out_shape=tuple((jax.ShapeDtypeStruct(r.shape,...]
where the time goes in v2:
time: 99 us; the launch traced here: 98.9 us
  Pallas kernels  98.1 us (99%)
    pallas_call x1, Pallas kernels, per_device(): pl.pallas_call(functools.partial(kernel, nz, nsec, ntp, n_sems), out_shap...  96 us
    pallas_call x1, Pallas kernels, per_device(): pl.pallas_call(write_out, out_shape=tuple((jax.ShapeDtypeStruct(r.shape,...  2.09 us

profile of v2, /device:TPU:1, one launch (start us, length us, event | category | flops | bytes accessed | tf_op | source)
XLA Modules:
  0.0 98.9 jit_solution(6241321541148915676)
XLA Ops:
  0.6 96.0 %shard_map.170 = (bf16[512,128]{1,0:T(8,128)(2,1)}, bf16[512,128]{1,0:T(8,128)(2,1)}, bf16[512,128]{1,0:T(8,128)(2,1)}, bf16[512,128]{1,0:T(8,128)(2,1)}, bf16[5...) custom-call(s32[64]{0:T(128)} %bs.1, ...), custom_call_target="tpu_custom_call" | custom-call | flops 8999999488 | bytes 4000000 | tf_op jit(solution)/shard_map/pallas_call | solution.py:486
  96.7 2.1 %shard_map.171 = (bf16[512,128]{1,0:T(8,128)(2,1)}, bf16[512,128]{1,0:T(8,128)(2,1)}, bf16[512,128]{1,0:T(8,128)(2,1)}, bf16[512,128]{1,0:T(8,128)(2,1)}, bf16[5...) custom-call(bf16[512,128]{1,0:T(8,128)(2,1)} %get-tuple-element.16.refs_0_, ...), custom_call_target="tpu_custom_call" | custom-call | tf_op jit(solution)/shard_map/pallas_call | solution.py:530

commit v3 on v2

--- a/solution.py
+++ b/solution.py
@@ -310,12 +310,12 @@
     ring_arrive(mb, mb_ids, half, EARLY)
     for g in range(1, n_groups):
         cross_forward(g)
+    combine(SELF)
     send_partial(CROSS)
-    combine(SELF)
+    norm(SELF, self_out)
     combine(CROSS)
-    norm(SELF, self_out)
-
-    def backward(a, h, keys, values, keys_t, slot, into):
+
+    def backward(a, h, keys, values, keys_t, slot, keep):
         dk = dv = None
         for t in range(rows // TQ):
             cols = slice(t * TQ, (t + 1) * TQ)
@@ -334,16 +334,28 @@
             dv = dv_t if dv is None else dv + dv_t
             dk = dk_t if dk is None else dk + dk_t
             dq[a, h, :, cols] = dq[a, h, :, cols] + dot(keys_t, ds, 1, 0)
-        kacc[into, 0] = kacc[into, 0] + dk * SCALE
-        kacc[into, 1] = kacc[into, 1] + dv
-
-    def self_backward(slot, h, into):
-        backward(SELF, h, kv[slot, 0], kv[slot, 1], kv[slot, 0].T, slot, into)
+        keep(0, dk * SCALE)
+        keep(1, dv)
+
+    def self_backward(offset, h, first):
+        slot = lax.rem(z + offset, nz)
+
+        def keep(j, value):
+            kacc[offset, j] = value if first else kacc[offset, j] + value
+
+        backward(SELF, h, kv[slot, 0], kv[slot, 1], kv[slot, 0].T, slot, keep)
+
+    def back_blocks(count, start, step, first):
+        def one(i, c):
+            self_backward(lax.rem(start + i * step, nz), x if first else 1 - x, first)
+            return c
+
+        lax.fori_loop(0, count, one, 0)
 
     rs_ids, mrs_ids = ring_ids(), ring_ids()
 
-    def reduce_step(dist, part, recv, snd, ids):
-        for d, j in LATE + EARLY:
+    def reduce_step(dist, part, recv, snd, ids, pairs):
+        for d, j in pairs:
             if (dist, d, j) in ids:
                 own = part(d, j)
                 if (dist + 1, d, j) in ids:
@@ -356,72 +368,57 @@
         arrive(do.at[a, 1 - x], do_ids[a][0], partner)
         arrive(dstat.at[a, 1 - x], do_ids[a][1], partner)
 
-    def cross_backward():
+    def cross_backward(first):
         def one(g, c):
-            kacc[0] = jnp.zeros_like(kacc[0])
-            keys_t = cross_group(g, 0).T
-
-            def each(h, c2):
-                backward(CROSS, h, cross_group(g, 0), cross_group(g, 1), keys_t, None, 0)
-                return c2
-
-            lax.fori_loop(0, 2, each, 0)
-            for j in range(2):
-                ms[pl.ds(g * per, per), j] = kacc[0, j].reshape(per, srows, HEAD_DIM)
+            def keep(j, value):
+                at = pl.ds(g * per, per)
+                value = value.reshape(per, srows, HEAD_DIM)
+                ms[at, j] = value if first else ms[at, j] + value
+
+            keys = cross_group(g, 0)
+            backward(CROSS, x if first else 1 - x, keys, cross_group(g, 1), keys.T, None, keep)
             return c
 
         lax.fori_loop(0, n_groups, one, 0)
 
-    def mem_own(dist, d, j):
-        return ms[((dist if d == 0 else nz - dist) + 1) % nz, j]
-
     def mem_step(dist):
-        reduce_step(dist, functools.partial(mem_own, dist), mrs_r, mrs_s, mrs_ids)
-
-    def self_step(dist):
-        reduce_step(dist, lambda d, j: kacc[0 if dist == half else 1 + d, j], rs_r, rs_s, rs_ids)
-
-    def back_pair(dist, halves):
-        def one(i, c):
-            d, h = i // len(halves), i % len(halves)
-            h = halves[0] if len(halves) == 1 else h
-            self_backward(zoff((1 - 2 * d) * dist), h, 1 + d)
-            return c
-
-        lax.fori_loop(0, 2 * len(halves), one, 0)
-
-    kacc[...] = jnp.zeros_like(kacc)
-    self_backward(zoff(half), x, 0)
+        def part(d, j):
+            return ms[((dist if d == 0 else nz - dist) + 1) % nz, j]
+
+        reduce_step(dist, part, mrs_r, mrs_s, mrs_ids, LATE + EARLY)
+
+    def self_step(dist, pairs):
+        reduce_step(dist, lambda d, j: kacc[dist if d == 0 else nz - dist, j], rs_r, rs_s, rs_ids, pairs)
+
+    def send_query(a):
+        dqs[a] = dq[a, 1 - x].astype(BF16)
+        send(dqs.at[a], dqr.at[a], dq_ids[a], partner)
+
+    back_blocks(3, half - 1, 1, True)
+    for dist in range(half - 2, 1, -1):
+        back_blocks(2, dist, nz - 2 * dist, True)
+    do_arrive(SELF)
+    back_blocks(1, half, 1, False)
+    self_step(half, EARLY)
     norm(CROSS, cross_out)
-    back_pair(half - 1, (x,))
-    do_arrive(SELF)
-    self_backward(zoff(half), 1 - x, 0)
-    self_step(half)
-    back_pair(half - 1, (1 - x,))
-    self_step(half - 1)
+    back_blocks(2, half - 1, 2, False)
+    self_step(half - 1, LATE)
+    back_blocks(3, nz - 1, 1, True)
+    cross_backward(True)
+    self_step(half - 1, EARLY)
     do_arrive(CROSS)
-    cross_backward()
+    cross_backward(False)
     mem_step(half)
-    dqs[CROSS] = dq[CROSS, 1 - x].astype(BF16)
-    send(dqs.at[CROSS], dqr.at[CROSS], dq_ids[CROSS], partner)
-    for dist in range(half - 2, 0, -1):
-        if dist == 1:
-            kacc[0] = jnp.zeros_like(kacc[0])
-
-            def back_own(h, c):
-                self_backward(z, h, 0)
-                return c
-
-            lax.fori_loop(0, 2, back_own, 0)
-            mem_step(2)
-        kacc[1:3] = jnp.zeros_like(kacc[1:3])
-        back_pair(dist, (0, 1))
-        self_step(dist)
-        if dist > 1:
-            mem_step(dist + 1)
-    dqs[SELF] = dq[SELF, 1 - x].astype(BF16)
-    send(dqs.at[SELF], dqr.at[SELF], dq_ids[SELF], partner)
+    send_query(CROSS)
+    for dist in range(half - 2, 1, -1):
+        back_blocks(2, dist, nz - 2 * dist, False)
+        mem_step(dist + 1)
+        self_step(dist, LATE + EARLY)
+    mem_step(2)
+    back_blocks(3, nz - 1, 1, False)
+    send_query(SELF)
     mem_step(1)
+    self_step(1, LATE + EARLY)
 
     def reduced(own, recv, ids, j):
         for d in range(2):
@@ -458,16 +455,12 @@
 
 
 def write_out(*refs):
-    sems, stage = refs[-1], refs[16:24]
-    ins = [pltpu.make_async_copy(refs[i], stage[i], sems.at[0, i]) for i in range(8)]
-    outs = [pltpu.make_async_copy(stage[i], refs[8 + i], sems.at[1, i]) for i in range(8)]
-    for c in ins:
+    sems = refs[-1]
+    copies = [pltpu.make_async_copy(refs[i], refs[8 + i], sems.at[i]) for i in range(8)]
+    for c in copies:
         c.start()
-    for c, d in zip(ins, outs):
+    for c in copies:
         c.wait()
-        d.start()
-    for d in outs:
-        d.wait()
 
 
 def per_device(nz, nsec, ntp, *args):
@@ -480,9 +473,8 @@
     hbm = pl.BlockSpec(memory_space=pltpu.HBM)
     vmem = pl.BlockSpec(memory_space=pltpu.VMEM)
     smem = pl.BlockSpec(memory_space=pltpu.SMEM)
-    frame = jax.ShapeDtypeStruct((rows, HEAD_DIM), BF16)
-    memory = jax.ShapeDtypeStruct(mk.shape, BF16)
     V = pltpu.VMEM
+    frame, memory = V((rows, HEAD_DIM), BF16), V(mk.shape, BF16)
     results = pl.pallas_call(
         functools.partial(kernel, nz, nsec, ntp, n_sems),
         out_shape=(frame, frame, frame, frame, frame, frame, memory, memory),
@@ -507,7 +499,7 @@
             V((2, 2, HEAD_DIM, rows), F32),
             V((2, HEAD_DIM, rows), BF16),
             V((2, HEAD_DIM, rows), BF16),
-            V((3, 2, rows, HEAD_DIM), F32),
+            V((nz, 2, rows, HEAD_DIM), F32),
             V((2, half, 2, rows, HEAD_DIM), BF16),
             V((2, half, 2, rows, HEAD_DIM), BF16),
             V((nz, 2, srows, HEAD_DIM), F32),
@@ -526,14 +518,13 @@
         ),
         cost_estimate=pl.CostEstimate(flops=9_000_000_000, bytes_accessed=4_000_000, transcendentals=10_000_000),
     )(bs, sq, sk, sv, sgain.reshape(1, -1), sgrad, cq, mk, mv, cgain.reshape(1, -1), cgrad)
-    spec = pl.BlockSpec(memory_space=pl.ANY)
     return pl.pallas_call(
         write_out,
         out_shape=tuple(jax.ShapeDtypeStruct(r.shape, r.dtype) for r in results),
-        in_specs=[spec] * 8,
-        out_specs=(spec,) * 8,
-        scratch_shapes=[V(r.shape, r.dtype) for r in results] + [pltpu.SemaphoreType.DMA((2, 8))],
-        compiler_params=pltpu.CompilerParams(vmem_limit_bytes=56 * 1024 * 1024),
+        in_specs=[vmem] * 8,
+        out_specs=(pl.BlockSpec(memory_space=pl.ANY),) * 8,
+        scratch_shapes=[pltpu.SemaphoreType.DMA((8,))],
+        compiler_params=pltpu.CompilerParams(vmem_limit_bytes=32 * 1024 * 1024),
     )(*results)
 
 

time: 99 us -> 91.4 us (0.923)
  Pallas kernels: 98.1 us -> 90.5 us
    pallas_call x1, Pallas kernels: 96 us -> 89.5 us  [per_device(): pl.pallas_call(functools.partial(kernel, nz, nsec, ntp, n_sems), out_shap...]
    pallas_call x1, Pallas kernels: 2.09 us -> 1.03 us  [per_device(): pl.pallas_call(write_out, out_shape=tuple((jax.ShapeDtypeStruct(r.shape,...]
where the time goes in v3:
time: 91.4 us; the launch traced here: 91.3 us
  Pallas kernels  90.5 us (99%)
    pallas_call x1, Pallas kernels, per_device(): pl.pallas_call(functools.partial(kernel, nz, nsec, ntp, n_sems), out_shap...  89.5 us

profile of v3, /device:TPU:1, one launch (start us, length us, event | category | flops | bytes accessed | tf_op | source)
XLA Modules:
  0.0 91.3 jit_solution(14622746124650565425)
XLA Ops:
  0.6 89.5 %shard_map.170 = (bf16[512,128]{1,0:T(8,128)(2,1)S(1)}, bf16[512,128]{1,0:T(8,128)(2,1)S(1)}, bf16[512,128]{1,0:T(8,128)(2,1)S(1)}, bf16[512,128]{1,0:T(8,128)(2...) custom-call(s32[64]{0:T(128)} %bs.1, ...), custom_call_target="tpu_custom_call" | custom-call | flops 8999999488 | bytes 4000000 | tf_op jit(solution)/shard_map/pallas_call | solution.py:478
  90.1 1.0 %shard_map.171 = (bf16[512,128]{1,0:T(8,128)(2,1)}, bf16[512,128]{1,0:T(8,128)(2,1)}, bf16[512,128]{1,0:T(8,128)(2,1)}, bf16[512,128]{1,0:T(8,128)(2,1)}, bf16[5...) custom-call(bf16[512,128]{1,0:T(8,128)(2,1)S(1)} %get-tuple-element.16.refs_, ...), custom_call_target="tpu_custom_call" | custom-call | tf_op jit(solution)/shard_map/pallas_call | solution.py:521

commit v4 on v3

--- a/solution.py
+++ b/solution.py
@@ -240,7 +240,8 @@
         ring_pass(kv, kv_ids, s, LATE)
         if s > 1:
             both_halves(zoff(s - 1))
-        ring_pass(mb, mb_ids, s, EARLY + LATE)
+        if s < half - 1:
+            ring_pass(mb, mb_ids, s, EARLY + LATE)
         if s == 1:
             dq[...] = jnp.zeros_like(dq)
             for a in (SELF, CROSS):
@@ -250,6 +251,7 @@
     both_halves(zoff(1 - half))
     both_halves(zoff(half - 1))
     ring_arrive(kv, kv_ids, half, EARLY)
+    ring_pass(mb, mb_ids, half - 1, EARLY + LATE)
     self_forward(zoff(half), 1 - x)
 
     o_ids = [(sem_id(), sem_id()) for _ in range(2)]
@@ -397,24 +399,24 @@
     back_blocks(3, half - 1, 1, True)
     for dist in range(half - 2, 1, -1):
         back_blocks(2, dist, nz - 2 * dist, True)
+    norm(CROSS, cross_out)
     do_arrive(SELF)
     back_blocks(1, half, 1, False)
     self_step(half, EARLY)
-    norm(CROSS, cross_out)
     back_blocks(2, half - 1, 2, False)
     self_step(half - 1, LATE)
-    back_blocks(3, nz - 1, 1, True)
     cross_backward(True)
-    self_step(half - 1, EARLY)
     do_arrive(CROSS)
     cross_backward(False)
     mem_step(half)
+    self_step(half - 1, EARLY)
     send_query(CROSS)
     for dist in range(half - 2, 1, -1):
         back_blocks(2, dist, nz - 2 * dist, False)
         mem_step(dist + 1)
         self_step(dist, LATE + EARLY)
     mem_step(2)
+    back_blocks(3, nz - 1, 1, True)
     back_blocks(3, nz - 1, 1, False)
     send_query(SELF)
     mem_step(1)
@@ -440,10 +442,10 @@
         send(mfin.at[:, src_rows, :], mout.at[:, :, own_cols], ret_ids[k - 1], to)
     mine = pltpu.make_async_copy(mfin.at[:, own_rows, :], mout.at[:, :, own_cols], lsem.at[0])
     mine.start()
+    finish_query(SELF, query_grad)
+    mine.wait()
     key_grad[...] = reduced(kacc[0, 0], rs_r, rs_ids, 0)
     value_grad[...] = reduced(kacc[0, 1], rs_r, rs_ids, 1)
-    finish_query(SELF, query_grad)
-    mine.wait()
     for k in range(1, n_peers):
         fs, ft = lax.rem(sec + nsec - k // ntp, nsec), lax.rem(tp + ntp - k % ntp, ntp)
         cols = pl.ds(pl.multiple_of((fs * ntp + ft) * HEAD_DIM, HEAD_DIM), HEAD_DIM)

time: 91.4 us -> 90.5 us (level)
    pallas_call x1, Pallas kernels: 89.5 us -> 88.5 us  [per_device(): pl.pallas_call(functools.partial(kernel, nz, nsec, ntp, n_sems), out_shap...]
where the time goes in v4:
time: 90.5 us; the launch traced here: 90.4 us
  Pallas kernels  89.6 us (99%)
    pallas_call x1, Pallas kernels, per_device(): pl.pallas_call(functools.partial(kernel, nz, nsec, ntp, n_sems), out_shap...  88.5 us

profile of v4, /device:TPU:1, one launch (start us, length us, event | category | flops | bytes accessed | tf_op | source)
XLA Modules:
  0.0 90.4 jit_solution(8863618801902483623)
XLA Ops:
  0.6 88.5 %shard_map.170 = (bf16[512,128]{1,0:T(8,128)(2,1)S(1)}, bf16[512,128]{1,0:T(8,128)(2,1)S(1)}, bf16[512,128]{1,0:T(8,128)(2,1)S(1)}, bf16[512,128]{1,0:T(8,128)(2...) custom-call(s32[64]{0:T(128)} %bs.1, ...), custom_call_target="tpu_custom_call" | custom-call | flops 8999999488 | bytes 4000000 | tf_op jit(solution)/shard_map/pallas_call | solution.py:480
  89.2 1.0 %shard_map.171 = (bf16[512,128]{1,0:T(8,128)(2,1)}, bf16[512,128]{1,0:T(8,128)(2,1)}, bf16[512,128]{1,0:T(8,128)(2,1)}, bf16[512,128]{1,0:T(8,128)(2,1)}, bf16[5...) custom-call(bf16[512,128]{1,0:T(8,128)(2,1)S(1)} %get-tuple-element.16.refs_, ...), custom_call_target="tpu_custom_call" | custom-call | tf_op jit(solution)/shard_map/pallas_call | solution.py:523

commit v5 on v4

--- a/solution.py
+++ b/solution.py
@@ -13,7 +13,7 @@
 NEG = -1e30
 SCALE = 1.0 / math.sqrt(HEAD_DIM)
 C2 = SCALE * math.log2(math.e)
-TQ = 256
+TQ = 512
 MESH = pl.DeviceIdType.MESH
 F32 = jnp.float32
 BF16 = jnp.bfloat16
@@ -156,9 +156,11 @@
             i = sem_id()
             send(src.at[:, cols], mb.at[z, j, own_rows, :], i, to)
             mem_ids.append((o, j, i))
-    for pairs in (EARLY, LATE):
+    def first_send(pairs):
         for d, j in pairs:
             send((k_in, v_in)[j], kv.at[z, j], kv_ids[1, d, j], neighbour[d])
+
+    first_send(EARLY)
     q_ids = [sem_id(), sem_id()]
     for a, src in enumerate((q_in, cq_in)):
         send(src, qs.at[a, x], q_ids[a], partner)
@@ -223,6 +225,7 @@
     for c in local[:3]:
         c.wait()
     self_forward(z, x)
+    first_send(LATE)
     for c in local[3:]:
         c.wait()
     for o, j, i in mem_ids:

time: 90.5 us -> 90.1 us (level)
  no operation moved by 1% of the time
where the time goes in v5:
time: 90.1 us; the launch traced here: 90 us
  Pallas kernels  89.4 us (99%)
    pallas_call x1, Pallas kernels, per_device(): pl.pallas_call(functools.partial(kernel, nz, nsec, ntp, n_sems), out_shap...  88.3 us

profile of v5, /device:TPU:1, one launch (start us, length us, event | category | flops | bytes accessed | tf_op | source)
XLA Modules:
  0.0 90.0 jit_solution(3389170718652963670)
XLA Ops:
  0.6 88.3 %shard_map.170 = (bf16[512,128]{1,0:T(8,128)(2,1)S(1)}, bf16[512,128]{1,0:T(8,128)(2,1)S(1)}, bf16[512,128]{1,0:T(8,128)(2,1)S(1)}, bf16[512,128]{1,0:T(8,128)(2...) custom-call(s32[64]{0:T(128)} %bs.1, ...), custom_call_target="tpu_custom_call" | custom-call | flops 8999999488 | bytes 4000000 | tf_op jit(solution)/shard_map/pallas_call | solution.py:483
  89.0 1.0 %shard_map.171 = (bf16[512,128]{1,0:T(8,128)(2,1)}, bf16[512,128]{1,0:T(8,128)(2,1)}, bf16[512,128]{1,0:T(8,128)(2,1)}, bf16[512,128]{1,0:T(8,128)(2,1)}, bf16[5...) custom-call(bf16[512,128]{1,0:T(8,128)(2,1)S(1)} %get-tuple-element.16.refs_, ...), custom_call_target="tpu_custom_call" | custom-call | tf_op jit(solution)/shard_map/pallas_call | solution.py:526
